TPU v7x, 512 devices: a whole 4x8x8 slice. The times are simulated.
512 devices in a mesh: inst: 8 (over y), tm: 16 (over z, core), filt: 4 (over x).
Axes of the slice: x: 4, y: 8, z: 8, core: 2. Of those that a mesh axis runs over, the one named last changes fastest.
Arguments:
- activations: bfloat16 [32, 7680, 256], P('inst', 'tm'), may hold values from -6 to 6
- conv_weight: bfloat16 [2304, 512], P(None, 'filt'), may hold values from -0.125 to 0.125
- class_weight: float32 [512, 5], P('filt'), may hold values from -1.2 to 1.2
- class_bias: float32 [5], replicated, may hold values from -4 to 4
- teacher_logits: float32 [32, 64, 5], P('inst', 'tm'), may hold values from -15 to 300
- night_of: int32 [32], P('inst'), may hold values from 0 to 7, never falling along the last dimension, each value on 1 to 8 neighbouring positions
- section_labels: int32 [8, 64], P(None, 'tm'), may hold values from 0 to 4
Outputs:
- student_logits: float32 [32, 64, 5], P('inst', 'tm')
- grad_weight: float32 [2304, 512], P(('inst', 'tm'), 'filt')
Inputs may be any that keep to these rules, and one draw needn't show every extreme that they name: `night_of`: instances of one night stand in a row, each night has 1 to 8 of them and some night has 8.
All inputs are finite; a program needn't handle non-finite values.
Results may differ from a plain program's by a relative error of at most 0.0011.
Values may be sent and summed in bfloat16 or wider, within the bound.
A program may use at most 64 MiB of HBM per device.

v0:
```python
import jax
import jax.numpy as jnp
from jax import lax
from jax.sharding import PartitionSpec as P

EPOCH = 120


def padded_2(block, sides, width):
    for axis, dim in sides:
        count = lax.axis_size(axis)
        forward = [(i, i + 1) for i in range(count - 1)]
        backward = [(target, source) for source, target in forward]
        low = lax.ppermute(
            lax.slice_in_dim(block, block.shape[dim] - width, None, axis=dim), axis, forward
        )
        high = lax.ppermute(lax.slice_in_dim(block, 0, width, axis=dim), axis, backward)
        block = jnp.concatenate([low, block, high], axis=dim)
    return block


def local(
    activations, conv_weight, class_weight, class_bias, teacher_logits, night_of, section_labels
):
    inst_rows, time_rows, channels = activations.shape
    filters = conv_weight.shape[1]
    tap_count = conv_weight.shape[0] // channels
    margin = tap_count // 2
    classes = class_weight.shape[1]
    night_count = section_labels.shape[0]
    padded = padded_2(activations, (("tm", 1),), margin)
    kernel = conv_weight.reshape(tap_count, channels, filters)
    flat_rows = inst_rows * time_rows
    summed = jnp.zeros((flat_rows, filters), jnp.float32)
    for offset in range(tap_count):
        window = padded[:, offset : offset + time_rows, :].reshape(flat_rows, channels)
        summed = summed + jnp.dot(window, kernel[offset], preferred_element_type=jnp.float32)
    pre = summed.reshape(inst_rows, time_rows, filters)
    act = jnp.where(pre > 0, pre, jnp.expm1(pre))
    epoch_count = time_rows // EPOCH
    pooled = act.reshape(inst_rows, epoch_count, EPOCH, filters).mean(axis=2)
    logit_part = jnp.einsum("ief,fs->ies", pooled, class_weight, precision=lax.Precision.HIGHEST)
    logits = lax.psum(logit_part, "filt") + class_bias
    teacher = jax.nn.softmax(teacher_logits, axis=-1)
    member = (night_of[:, None] == jnp.arange(night_count, dtype=jnp.int32)[None, :]).astype(
        jnp.float32
    )
    local_totals = jnp.einsum("in,ies->nes", member, teacher, precision=lax.Precision.HIGHEST)
    local_counts = jnp.sum(member, axis=0)
    totals, counts = lax.psum((local_totals, local_counts), "inst")
    ensemble = totals / counts[:, None, None]
    soft_target = jnp.einsum("in,nes->ies", member, ensemble, precision=lax.Precision.HIGHEST)
    label_hot = (
        section_labels[:, :, None] == jnp.arange(classes, dtype=jnp.int32)[None, None, :]
    ).astype(jnp.float32)
    hard_target = jnp.einsum("in,nes->ies", member, label_hot, precision=lax.Precision.HIGHEST)
    target = 0.5 * soft_target + 0.5 * hard_target
    expo = jnp.exp(logits)
    student = expo / jnp.sum(expo, axis=-1, keepdims=True)
    slope = jnp.einsum(
        "ies,fs->ief", student - target, class_weight, precision=lax.Precision.HIGHEST
    )
    spread = jnp.broadcast_to(
        slope[:, :, None, :], (inst_rows, epoch_count, EPOCH, filters)
    ).reshape(inst_rows, time_rows, filters)
    deriv = jnp.where(pre > 0, 1.0, jnp.exp(pre))
    upstream = (spread * deriv).astype(jnp.bfloat16).reshape(flat_rows, filters)
    grads = []
    for offset in range(tap_count):
        window = padded[:, offset : offset + time_rows, :].reshape(flat_rows, channels)
        grads.append(jnp.einsum("rc,rf->cf", window, upstream, preferred_element_type=jnp.float32))
    stacked = jnp.concatenate(grads, axis=0)
    reduced = lax.psum_scatter(stacked, ("inst", "tm"), scatter_dimension=0, tiled=True)
    grad_weight = reduced / (inst_rows * lax.axis_size("inst"))
    return (logits, grad_weight)


def solution(mesh):
    in_specs = (
        P("inst", "tm", None),
        P(None, "filt"),
        P("filt", None),
        P(),
        P("inst", "tm", None),
        P("inst"),
        P(None, "tm"),
    )
    out_specs = (P("inst", "tm", None), P(("inst", "tm"), "filt"))
    return jax.shard_map(local, mesh=mesh, in_specs=in_specs, out_specs=out_specs, check_vma=False)
```

profile of v0, /device:TPU:1, one launch (start us, length us, event | category | flops | bytes accessed | tf_op | source)
XLA Modules:
  0.0 287.9 jit_solution(1886132758671391222)
XLA Ops:
  7.2 0.0 copy-start
  7.2 0.0 copy-start.13
  7.2 0.0 copy-start.12
  7.2 0.0 all-reduce.4.cloned.1.call-start
  7.2 0.7 fusion.63
  8.0 5.4 %collective-permute-start = (bf16[4,4,256]{2,1,0:T(4,128)(2,1)S(1)}, bf16[4,4,256]{2,1,0:T(4,128)(2,1)S(1)}, u32[]{:S(2)}, u32[]{:S(2)}) collective-permute-start(bf16[4,4,256]{2,1,0:T(4,128)(2,1)S(1)} %get-tuple-element.15), channel_id=1, source_target_pairs={{0,4},{4,8},{8,12},{12,16},{16,20},{20,24},{24,28},{28,32},{32,36}... | collective-permute-start | bytes 24584 | tf_op jit(solution)/shard_map/ppermute | solution.py:14
  13.4 4.7 %collective-permute-start.1 = (bf16[4,4,256]{2,1,0:T(4,128)(2,1)S(1)}, bf16[4,4,256]{2,1,0:T(4,128)(2,1)S(1)}, u32[]{:S(2)}, u32[]{:S(2)}) collective-permute-start(bf16[4,4,256]{2,1,0:T(4,128)(2,1)S(1)} %get-tuple-element.16), channel_id=1, source_target_pairs={{4,0},{8,4},{12,8},{16,12},{20,16},{24,20},{28,24},{32,28},{36,32}... | collective-permute-start | bytes 24584 | tf_op jit(solution)/shard_map/ppermute | solution.py:17
  18.1 0.9 fusion.64
  19.0 0.7 convert_reduce_fusion
  19.8 0.1 broadcast_divide_fusion
  19.9 1.0 fusion.39
  20.9 2.6 fusion.28
  23.4 20.3 %all-reduce.1 = (f32[8,4,5]{2,0,1:T(8,128)S(1)}, f32[8]{0:T(128)S(1)}) all-reduce(f32[8,4,5]{2,0,1:T(8,128)S(1)} %fusion.39, f32[8]{0:T(128)S(1)} %convert_reduce_fusion), channel_id=1, replica_groups=mesh['inst'=8,'tm'=16,'filt'=4] {'inst'}, use_global_device_ids=true, to_apply=%region_5.6 | all-reduce | flops 168 | bytes 1344 | tf_op jit(solution)/shard_map/psum | solution.py:50
  43.8 0.0 copy-done.13
  43.8 0.2 fusion.35
  44.0 0.0 copy-done.12
  44.0 0.2 fusion.37
  44.2 0.0 collective-permute-done
  44.2 0.0 copy-done.1
  44.2 0.9 pad_maximum_fusion
  45.1 0.0 copy-start.2
  45.1 0.0 copy-start.4
  45.1 0.0 copy-start.6
  45.1 0.1 copy-done.9
  45.3 0.4 fusion.32
  45.7 0.0 collective-permute-done.1
  45.7 0.4 copy-done.2
  46.1 0.9 fusion.62
  47.0 0.4 fusion.21
  47.4 0.4 fusion.23
  47.8 0.4 fusion.25
  48.2 0.0 copy-done.4
  48.3 0.4 convolution_add_fusion.3
  48.7 0.0 copy-start.8
  48.7 0.4 convolution_add_fusion.2
  49.1 0.0 copy-done.6
  49.1 0.8 copy-done.8
  49.9 0.4 fusion.4
  50.3 0.0 copy-start.11
  50.3 1.4 exponential_select_fusion
  51.7 0.4 fusion.19
  52.1 0.0 copy-done
  52.1 0.2 fusion.43
  52.3 8.7 %psum.21 = f32[4,4,5]{2,1,0:T(4,128)S(1)} all-reduce(f32[4,4,5]{2,1,0:T(4,128)S(1)} %fusion.43), channel_id=1, replica_groups=mesh['inst'=8,'tm'=16,'filt'=4] {'filt'}, use_global_device_ids=true, to_apply=%region_1.2 | all-reduce | flops 80 | bytes 640 | tf_op jit(solution)/shard_map/psum | solution.py:43
  60.9 0.0 copy-done.11
  60.9 0.1 exponential_reduce_fusion
  61.0 0.2 fusion.45
  61.3 1.4 fusion.20
  62.7 0.0 copy-done.5
  62.7 1.1 fusion.13
  63.8 0.0 copy-done.3
  63.8 1.1 fusion.12
  64.9 1.1 fusion.11
  66.1 0.1 copy-done.7
  66.1 1.1 fusion.10
  67.2 1.2 fusion.9
  68.4 1.1 fusion.8
  69.5 1.1 fusion.7
  70.6 1.1 fusion.6
  71.8 1.1 fusion.5
  72.9 0.0 all-reduce.4.cloned.1.call-update
  72.9 1.3 dynamic-slice
  74.9 204.8 %all-reduce.4.cloned.1.call-done = f32[2304,128]{1,0:T(8,128)} async-done(((f32[2304,128]{1,0:T(8,128)}), f32[2304,128]{1,0:T(8,128)}) %all-reduce.4.cloned.1.call-update) | async-done | bytes 1179664
  279.7 1.3 dynamic-slice_multiply_fusion
  (8 shorter events, 0.0 us)
Async XLA Ops:
  7.2 44.9 %copy-start = (f32[128,5]{0,1:T(8,128)S(1)}, f32[128,5]{0,1:T(8,128)}, u32[]{:S(2)}) copy-start(f32[128,5]{0,1:T(8,128)} %param.9) | copy-start | bytes 7684
  7.2 36.6 %copy-start.13 = (s32[4]{0:T(128)S(1)}, s32[4]{0:T(128)}, u32[]{:S(2)}) copy-start(s32[4]{0:T(128)} %param.12) | copy-start | bytes 52
  7.2 36.8 %copy-start.12 = (s32[8,4]{0,1:T(4,128)S(1)}, s32[8,4]{0,1:T(4,128)}, u32[]{:S(2)}) copy-start(s32[8,4]{0,1:T(4,128)} %param.13) | copy-start | bytes 388
  7.2 272.5 %all-reduce.4.cloned.1.call-start = ((), (), s32[]{:S(2)}) async-start(), calls=%async_computation | async-start | bytes 2359296
  8.0 36.2 %collective-permute-start = (bf16[4,4,256]{2,1,0:T(4,128)(2,1)S(1)}, bf16[4,4,256]{2,1,0:T(4,128)(2,1)S(1)}, u32[]{:S(2)}, u32[]{:S(2)}) collective-permute-start(bf16[4,4,256]{2,1,0:T(4,128)(2,1)S(1)} %get-tuple-element.15), channel_id=1, source_target_pairs={{0,4},{4,8},{8,12},{12,16},{16,20},{20,24},{24,28},{28,32},{32,36}... | collective-permute-start | bytes 24584 | tf_op jit(solution)/shard_map/ppermute | solution.py:14
  13.4 32.3 %collective-permute-start.1 = (bf16[4,4,256]{2,1,0:T(4,128)(2,1)S(1)}, bf16[4,4,256]{2,1,0:T(4,128)(2,1)S(1)}, u32[]{:S(2)}, u32[]{:S(2)}) collective-permute-start(bf16[4,4,256]{2,1,0:T(4,128)(2,1)S(1)} %get-tuple-element.16), channel_id=1, source_target_pairs={{4,0},{8,4},{12,8},{16,12},{20,16},{24,20},{28,24},{32,28},{36,32}... | collective-permute-start | bytes 24584 | tf_op jit(solution)/shard_map/ppermute | solution.py:17
  19.9 24.3 %copy-start.1 = (bf16[4,480,256]{2,1,0:T(8,128)(2,1)S(1)}, bf16[4,480,256]{2,1,0:T(8,128)(2,1)}, u32[]{:S(2)}) copy-start(bf16[4,480,256]{2,1,0:T(8,128)(2,1)} %param.7) | copy-start | bytes 2949124
  44.2 1.1 copy-start.9
  45.1 1.0 copy-start.2
  45.1 3.1 %copy-start.4 = (bf16[4,480,256]{2,1,0:T(8,128)(2,1)}, bf16[4,480,256]{2,1,0:T(8,128)(2,1)S(1)}, u32[]{:S(2)}) copy-start(bf16[4,480,256]{2,1,0:T(8,128)(2,1)S(1)} %get-tuple-element.11) | copy-start | bytes 2949124
  45.1 4.0 %copy-start.6 = (bf16[4,480,256]{2,1,0:T(8,128)(2,1)}, bf16[4,480,256]{2,1,0:T(8,128)(2,1)S(1)}, u32[]{:S(2)}) copy-start(bf16[4,480,256]{2,1,0:T(8,128)(2,1)S(1)} %get-tuple-element.10) | copy-start | bytes 2949124
  48.7 1.2 copy-start.8
  50.3 10.6 %copy-start.11 = (f32[5]{0:T(128)S(1)}, f32[5]{0:T(128)}, u32[]{:S(2)}) copy-start(f32[5]{0:T(128)} %param.10) | copy-start | bytes 64
  60.9 1.7 copy-start.5
  61.0 2.8 copy-start.10
  61.3 2.5 copy-start.3
  64.9 1.2 copy-start.7
Sparse Core Ops, SparseCore 0:
  73.1 206.5 all-reduce.3
where the time goes:
time: 288 us
  waiting for transfers between devices  205 us (71%)
  blocking collectives  29 us (10%)
  matrix products  18.8 us (7%)
  between operations  14.9 us (5%)
  starting transfers between devices  10.1 us (4%)
  other arithmetic  5.82 us (2%)
  local copies, waits for them, and re-layouts  4.35 us (2%)
    unnamed x2, waiting for transfers between devices  205 us
    psum x1, blocking collectives, local(): totals, counts = lax.psum((local_totals, local_counts), 'inst')  20.3 us
    dot_general x9, matrix products, local(): jnp.einsum('rc,rf->cf', window, upstream, preferred_element_type=jnp.floa...  10.2 us
    psum x1, blocking collectives, local(): logits = lax.psum(logit_part, 'filt') + class_bias  8.66 us
    dot_general x9, matrix products, local(): jnp.dot(window, kernel[offset], preferred_element_type=jnp.float32)  6.85 us
  transfers between devices with their start and end apart: 3, of which 1 were waited for; matrix products, arithmetic and copies ran while one was open for 3% of the time, Pallas kernels for 0%

commit v1 on v0

v1 whole, which is shorter than its diff:
```python
import functools

import jax
import jax.numpy as jnp
from jax import lax
from jax.experimental import pallas as pl
from jax.experimental.pallas import tpu as pltpu
from jax.sharding import PartitionSpec as P

f32, bf16, i32, i16 = jnp.float32, jnp.bfloat16, jnp.int32, jnp.int16
MESH = pl.DeviceIdType.MESH
EPOCH = 120
PAD = 16
UNIT = 36
WIDE = 2 * UNIT
WIDE_PAD = 80
SIXTEEN = False


def kernel(
    x, w, cw, tl, night, labels, bias,
    logits_out, grad_out,
    xp, wv, y_taps, deriv, pooled, up, xt, grad,
    teach, logit, half_tx, half_rx, total, tx, rx, piece, tx2, rx2,
    load_sem, halo_send, halo_recv, teach_send, teach_recv, logit_send, logit_recv,
    half_send, half_recv, send1, recv1, send2, recv2,
):
    yy, tm, xx = lax.axis_index("inst"), lax.axis_index("tm"), lax.axis_index("filt")
    zz, cc = tm // 2, tm % 2
    oc = 1 - cc
    ny, nz, nx = 8, 8, 4

    def remote(src, dst, ssem, rsem, dev):
        return pltpu.make_async_remote_copy(
            src_ref=src, dst_ref=dst, send_sem=ssem, recv_sem=rsem, device_id=dev, device_id_type=MESH
        )

    def arrived(dst, rsem):
        remote(dst, dst, rsem, rsem, (yy, tm, xx)).wait_recv()

    loads = [pltpu.make_async_copy(w, wv, load_sem.at[4])]
    loads += [
        pltpu.make_async_copy(x.at[i], xp.at[i, pl.ds(PAD, 480)], load_sem.at[i]) for i in range(4)
    ]
    for c in loads:
        c.start()

    barrier = pltpu.get_barrier_semaphore()

    def greet(dev):
        pl.semaphore_signal(barrier, inc=1, device_id=dev, device_id_type=MESH)

    greet((yy, zz * 2 + oc, xx))
    for d in range(1, 8):
        for c in range(2):
            greet((yy, lax.rem(zz + d, nz) * 2 + c, xx))
            greet((lax.rem(yy + d, ny), zz * 2 + c, xx))
    for d in range(1, 4):
        greet((yy, tm, lax.rem(xx + d, nx)))

    row = lax.broadcasted_iota(i32, (16, 128), 0)
    lane = lax.broadcasted_iota(i32, (16, 128), 1)
    t5 = jnp.concatenate([tl[i] for i in range(4)], axis=0)
    t5 = jnp.exp(t5 - jnp.max(t5, axis=1, keepdims=True))
    t5 = t5 / jnp.sum(t5, axis=1, keepdims=True)
    tile = jnp.zeros((16, 128), f32)
    for s in range(5):
        tile = jnp.where(lane == s, t5[:, s : s + 1], tile)
    for i in range(4):
        tile = jnp.where((lane == 8) & (row // 4 == i), night[i].astype(f32), tile)
    tile = jnp.where(lane == 9, 1.0, tile)
    teach[yy] = tile

    @pl.when(tm == 0)
    def _():
        for i in range(4):
            xp[i, 0:PAD, :] = jnp.zeros((PAD, 256), bf16)

    @pl.when(tm == 15)
    def _():
        for i in range(4):
            xp[i, PAD + 480 :, :] = jnp.zeros((PAD, 256), bf16)

    def weights(p):
        if p == 4:
            return wv[pl.ds(2048, 256), :]
        return jnp.concatenate([wv[pl.ds(512 * p, 256), :], wv[pl.ds(512 * p + 256, 256), :]], axis=1)

    def forward(i):
        for p in range(5):
            y = jnp.dot(xp[i, PAD : PAD + 480, :], weights(p), preferred_element_type=f32)
            y_taps[i, 2 * p, PAD : PAD + 480, :] = y[:, :128]
            if p < 4:
                y_taps[i, 2 * p + 1, PAD : PAD + 480, :] = y[:, 128:]

    loads[0].wait()
    loads[1].wait()
    forward(0)
    pl.semaphore_wait(barrier, 32)

    up_halo = remote(
        x.at[:, pl.ds(480 - PAD, PAD)], xp.at[:, pl.ds(0, PAD)], halo_send.at[0], halo_recv.at[0], (yy, tm + 1, xx)
    )
    down_halo = remote(
        x.at[:, pl.ds(0, PAD)], xp.at[:, pl.ds(PAD + 480, PAD)], halo_send.at[1], halo_recv.at[1], (yy, tm - 1, xx)
    )
    pl.when(tm < 15)(up_halo.start)
    pl.when(tm > 0)(down_halo.start)
    teach_copies = [
        remote(teach.at[yy], teach.at[yy], teach_send.at[d - 1], teach_recv.at[yy], (lax.rem(yy + d, ny), tm, xx))
        for d in range(1, 8)
    ]
    for c in teach_copies:
        c.start()

    for i in range(1, 4):
        loads[1 + i].wait()
        forward(i)

    pl.when(tm > 0)(up_halo.wait_recv)
    pl.when(tm < 15)(down_halo.wait_recv)
    xh = jnp.concatenate([xp[i, r : r + PAD, :] for i in range(4) for r in (0, PAD + 480)], axis=0)
    for p in range(5):
        y = jnp.dot(xh, weights(p), preferred_element_type=f32)
        for i in range(4):
            for h, r in enumerate((0, PAD + 480)):
                o = (2 * i + h) * PAD
                y_taps[i, 2 * p, r : r + PAD, :] = y[o : o + PAD, :128]
                if p < 4:
                    y_taps[i, 2 * p + 1, r : r + PAD, :] = y[o : o + PAD, 128:]

    for i in range(4):
        for e in range(4):
            o = PAD - 4 + EPOCH * e
            pre = y_taps[i, 0, pl.ds(o, EPOCH), :]
            for k in range(1, 9):
                pre = pre + y_taps[i, k, pl.ds(o + k, EPOCH), :]
            ex = jnp.exp(jnp.minimum(pre, 0.0))
            act = jnp.where(pre > 0, pre, ex - 1.0)
            deriv[i, pl.ds(EPOCH * e, EPOCH), :] = ex
            pooled[pl.ds(4 * i + e, 1), :] = jnp.sum(act, axis=0, keepdims=True) * (1.0 / EPOCH)

    cwt = cw[...]
    pool = pooled[...]
    part = jnp.zeros((16, 128), f32)
    for s in range(5):
        part = jnp.where(lane == s, jnp.sum(pool * cwt[s : s + 1, :], axis=1, keepdims=True), part)
    logit[xx] = part
    logit_copies = [
        remote(logit.at[xx], logit.at[xx], logit_send.at[d - 1], logit_recv.at[xx], (yy, tm, lax.rem(xx + d, nx)))
        for d in range(1, 4)
    ]
    for c in logit_copies:
        c.start()

    for i in range(4):
        xt[:, 512 * i : 512 * i + 512] = xp[i].T
    for d in range(1, 8):
        s = lax.rem(yy + d, ny)
        arrived(teach.at[s], teach_recv.at[s])
    nights = [night[i].astype(f32) for i in range(4)]
    sums = [jnp.zeros((16, 128), f32) for _ in range(4)]
    for j in range(8):
        t = teach[j]
        of = jnp.broadcast_to(t[:, 8:9], (16, 128))
        for i in range(4):
            sums[i] = sums[i] + jnp.where(of == nights[i], t, 0.0)
    soft = []
    for i in range(4):
        s = sums[i][0:4] + sums[i][4:8] + sums[i][8:12] + sums[i][12:16]
        soft.append(s / s[:, 9:10])
    soft = jnp.concatenate(soft, axis=0)
    label = jnp.zeros((16, 128), i32)
    for i in range(4):
        for e in range(4):
            label = jnp.where(row == 4 * i + e, labels[e, night[i]], label)
    target = 0.5 * soft + 0.5 * (lane == label).astype(f32)

    for d in range(1, 4):
        s = lax.rem(xx + d, nx)
        arrived(logit.at[s], logit_recv.at[s])
    logits = logit[0] + logit[1] + logit[2] + logit[3]
    for s in range(5):
        logits = logits + jnp.where(lane == s, bias[s], 0.0)
    for i in range(4):
        logits_out[i] = logits[4 * i : 4 * i + 4, :5]
    expo = jnp.where(lane < 5, jnp.exp(logits), 0.0)
    diff = expo / jnp.sum(expo, axis=1, keepdims=True) - target
    slope = jnp.zeros((16, 128), f32)
    for s in range(5):
        slope = slope + diff[:, s : s + 1] * cwt[s : s + 1, :]

    for i in range(4):
        up[i, 0:24, :] = jnp.zeros((24, 128), f32)
        up[i, 504:528, :] = jnp.zeros((24, 128), f32)
        for e in range(4):
            up[i, pl.ds(24 + EPOCH * e, EPOCH), :] = (
                deriv[i, pl.ds(EPOCH * e, EPOCH), :] * slope[4 * i + e : 4 * i + e + 1, :]
            )
    for p in range(5):
        acc = None
        for i in range(4):
            us = [up[i, pl.ds(12 - k, 512), :].astype(bf16) for k in range(2 * p, min(2 * p + 2, 9))]
            u = jnp.concatenate(us, axis=1) if p < 4 else us[0]
            g = jnp.dot(xt[:, 512 * i : 512 * i + 512], u, preferred_element_type=f32)
            acc = g if acc is None else acc + g
        grad[pl.ds(512 * p, 256), :] = acc[:, :128]
        if p < 4:
            grad[pl.ds(512 * p + 256, 256), :] = acc[:, 128:]

    def rows_of(j, h, core):
        if j < 8:
            return pl.ds(pl.multiple_of(core * 144, 8) + 288 * j + UNIT * (j % 2 + 2 * h), UNIT)
        z = j - 8
        return pl.ds(pl.multiple_of(core * 1152, 8) + 288 * (1 - z % 2 + 2 * h) + UNIT * z, UNIT)

    partner = (yy, zz * 2 + oc, xx)
    half_copies = []
    for part_at in range(2):
        for j in range(8 * part_at, 8 * part_at + 8):
            for h in range(2):
                half_tx[j, UNIT * h : UNIT * h + UNIT, :] = grad[rows_of(j, h, oc), :]
        sl = pl.ds(8 * part_at, 8)
        c = remote(half_tx.at[sl], half_rx.at[sl], half_send.at[part_at], half_recv.at[part_at], partner)
        c.start()
        half_copies.append(c)

    copies1 = []
    for part_at in range(2):
        half_copies[part_at].wait_recv()
        top = jnp.zeros((WIDE, 128), f32)
        for j in range(8 * part_at, 8 * part_at + 8):
            t = half_rx[j] + jnp.concatenate([grad[rows_of(j, h, cc), :] for h in range(2)], axis=0)
            total[j] = t
            top = jnp.maximum(top, jnp.abs(t))
        if SIXTEEN:
            top = jnp.max(top, axis=0, keepdims=True)
            power = jnp.ceil(jnp.log2(jnp.maximum(top, 1e-30)) + 0.01)
            factor = jnp.exp2(15.0 - power)
            power = jnp.broadcast_to(power, (WIDE_PAD - WIDE, 128))
            for j in range(8 * part_at, 8 * part_at + 8):
                q = jnp.concatenate([jnp.round(total[j] * factor), power], axis=0)
                tx[j] = q.astype(i32).astype(i16)
        else:
            for j in range(8 * part_at, 8 * part_at + 8):
                tx[j] = total[j]
        for d in range(1, 8):
            if part_at == 0:
                to, me = lax.rem(yy + d, ny), yy
                dev = (to, tm, xx)
            else:
                to, me = lax.rem(zz + d, nz), zz
                dev = (yy, to * 2 + cc, xx)
            base = 8 * part_at
            c = remote(
                tx.at[base + to], rx.at[base + me], send1.at[7 * part_at + d - 1], recv1.at[base + me], dev
            )
            c.start()
            copies1.append(c)

    copies2 = []
    for part_at in range(2):
        base = 8 * part_at
        me = yy if part_at == 0 else zz
        acc = total[base + me]
        for d in range(1, 8):
            s = base + lax.rem(me + d, 8)
            arrived(rx.at[s], recv1.at[s])
            t = rx[s].astype(f32)
            if SIXTEEN:
                t = t[:WIDE] * jnp.exp2(t[WIDE : WIDE + 1] - 15.0)
            acc = acc + t
        piece[part_at, 0:WIDE, :] = acc
        piece[part_at, WIDE:, :] = jnp.zeros((WIDE_PAD - WIDE, 128), f32)
        for m in range(4):
            tx2[4 * part_at + m] = piece[part_at, pl.ds(18 * m, 24), :]
        for m in range(4):
            h, c = m // 2, m % 2
            slot = 4 * part_at + m
            if part_at == 0:
                to, own = yy % 2 + 4 * cc + 2 * h, zz
                dev = (yy, to * 2 + c, xx)
                mine = (to == zz) & (cc == c)
            else:
                to, own = 4 * cc + 1 - zz % 2 + 2 * h, yy
                dev = (to, zz * 2 + c, xx)
                mine = (to == yy) & (cc == c)
            copy = remote(tx2.at[slot], rx2.at[own], send2.at[slot], recv2.at[own], dev)
            copies2.append((copy, mine))

            @pl.when(mine)
            def _():
                rx2[own] = tx2[slot]

            @pl.when(jnp.logical_not(mine))
            def _():
                copy.start()

    even = (yy + zz) % 2 == 0
    holder = jnp.where(even, zz // 4, yy // 4)
    place = jnp.where(even, zz, yy)
    for s in range(8):
        @pl.when(jnp.logical_not((place == s) & (holder == cc)))
        def _():
            arrived(rx2.at[s], recv2.at[s])
    out = rx2[0]
    for s in range(1, 8):
        out = out + rx2[s]
    grad_out[...] = out[:18] * (1.0 / 32)

    pl.when(tm < 15)(up_halo.wait_send)
    pl.when(tm > 0)(down_halo.wait_send)
    for c in teach_copies + logit_copies + half_copies + copies1:
        c.wait_send()
    for c, mine in copies2:
        pl.when(jnp.logical_not(mine))(c.wait_send)


def local(activations, conv_weight, class_weight, class_bias, teacher_logits, night_of, section_labels):
    vm = pl.BlockSpec(memory_space=pltpu.VMEM)
    sm = pl.BlockSpec(memory_space=pltpu.SMEM)
    hbm = pl.BlockSpec(memory_space=pltpu.HBM)
    wire, wire_rows = (i16, WIDE_PAD) if SIXTEEN else (f32, WIDE)
    dma = pltpu.SemaphoreType.DMA
    return pl.pallas_call(
        kernel,
        out_shape=(jax.ShapeDtypeStruct((4, 4, 5), f32), jax.ShapeDtypeStruct((18, 128), f32)),
        in_specs=[hbm, hbm, vm, vm, sm, sm, sm],
        out_specs=(vm, vm),
        scratch_shapes=[
            pltpu.VMEM((4, 512, 256), bf16),
            pltpu.VMEM((2304, 128), bf16),
            pltpu.VMEM((4, 9, 512, 128), f32),
            pltpu.VMEM((4, 480, 128), f32),
            pltpu.VMEM((16, 128), f32),
            pltpu.VMEM((4, 528, 128), f32),
            pltpu.VMEM((256, 2048), bf16),
            pltpu.VMEM((2304, 128), f32),
            pltpu.VMEM((8, 16, 128), f32),
            pltpu.VMEM((4, 16, 128), f32),
            pltpu.VMEM((16, WIDE, 128), f32),
            pltpu.VMEM((16, WIDE, 128), f32),
            pltpu.VMEM((16, WIDE, 128), f32),
            pltpu.VMEM((16, wire_rows, 128), wire),
            pltpu.VMEM((16, wire_rows, 128), wire),
            pltpu.VMEM((2, WIDE_PAD, 128), f32),
            pltpu.VMEM((8, 24, 128), f32),
            pltpu.VMEM((8, 24, 128), f32),
            dma((5,)),
            dma((2,)), dma((2,)),
            dma((7,)), dma((8,)),
            dma((3,)), dma((4,)),
            dma((2,)), dma((2,)),
            dma((14,)), dma((16,)),
            dma((8,)), dma((8,)),
        ],
        compiler_params=pltpu.CompilerParams(
            collective_id=0, has_side_effects=True, vmem_limit_bytes=48 << 20
        ),
    )(activations, conv_weight, class_weight.T, teacher_logits, night_of, section_labels.T, class_bias)


def solution(mesh):
    in_specs = (
        P("inst", "tm", None),
        P(None, "filt"),
        P("filt", None),
        P(),
        P("inst", "tm", None),
        P("inst"),
        P(None, "tm"),
    )
    out_specs = (P("inst", "tm", None), P(("inst", "tm"), "filt"))
    return jax.shard_map(local, mesh=mesh, in_specs=in_specs, out_specs=out_specs, check_vma=False)
```

time: 288 us -> 49.3 us (0.17)
  waiting for transfers between devices: 205 us -> 0 us
  Pallas kernels: 0 us -> 42.8 us
  blocking collectives: 29 us -> 0 us
  matrix products: 18.8 us -> 0 us
  between operations: 14.9 us -> 0.67 us
  starting transfers between devices: 10.1 us -> 0 us
  other arithmetic: 5.82 us -> 0 us
    unnamed x2 -> x0, waiting for transfers between devices: 205 us -> none
    pallas_call x0 -> x1, Pallas kernels: none -> 42.8 us  [local(): pl.pallas_call(kernel, out_shape=(jax.ShapeDtypeStruct((4, 4, 5), f32), j...]
    psum x2 -> x0, blocking collectives: 29 us -> none  [the longest x1 20.3 us: local(): totals, counts = lax.psum((local_totals, local_counts), 'inst')]
    dot_general x23 -> x0, matrix products: 18.8 us -> none  [the longest x9 10.2 us: local(): jnp.einsum('rc,rf->cf', window, upstream, preferred_element_type=jnp.floa...]
    ppermute x2 -> x0, starting transfers between devices: 10.1 us -> none  [the longest x1 5.39 us: padded_2(): lax.ppermute(lax.slice_in_dim(block, block.shape[dim] - width, None, axis...]
  transfers between devices with their start and end apart: 3 -> 0, of which waited for: 1 -> 0; matrix products, arithmetic and copies ran while one was open for 3% -> 0% of each run, Pallas kernels for 0% -> 0%
where the time goes in v1:
time: 49.3 us; the launch traced here: 49 us
  Pallas kernels  42.8 us (87%)
  local copies, waits for them, and re-layouts  5.51 us (11%)
  between operations  0.67 us (1%)
    pallas_call x1, Pallas kernels, local(): pl.pallas_call(kernel, out_shape=(jax.ShapeDtypeStruct((4, 4, 5), f32), j...  42.8 us
    unnamed x16, local copies, waits for them, and re-layouts  5.51 us

profile of v1, /device:TPU:1, one launch (start us, length us, event | category | flops | bytes accessed | tf_op | source)
XLA Modules:
  0.0 49.0 jit_solution(4030599862695536785)
XLA Ops:
  0.6 0.0 copy-start.4
  0.6 0.0 copy-start.5
  0.7 0.0 copy-start.6
  0.7 0.7 %copy-done.4 = s32[8,4]{0,1:T(4,128)S(1)} copy-done((s32[8,4]{0,1:T(4,128)S(1)}, s32[8,4]{0,1:T(4,128)}, u32[]{:S(2)}) %copy-start.4) | copy-done | bytes 152
  1.3 0.0 copy-done.5
  1.3 0.0 copy-done.6
  1.3 0.0 copy-start
  1.3 1.2 %copy-done = bf16[4,480,256]{2,1,0:T(8,128)(2,1)S(1)} copy-done((bf16[4,480,256]{2,1,0:T(8,128)(2,1)S(1)}, bf16[4,480,256]{2,1,0:T(8,128)(2,1)}, u32[]{:S(2)}) %copy-start) | copy-done | bytes 983064
  2.5 0.0 copy-start.1
  2.5 1.1 %copy-done.1 = bf16[2304,128]{1,0:T(8,128)(2,1)S(1)} copy-done((bf16[2304,128]{1,0:T(8,128)(2,1)S(1)}, bf16[2304,128]{1,0:T(8,128)(2,1)}, u32[]{:S(2)}) %copy-start.1) | copy-done | bytes 589848
  3.6 0.0 copy-start.2
  3.6 0.7 %copy-done.2 = f32[4,4,5]{2,1,0:T(4,128)S(1)} copy-done((f32[4,4,5]{2,1,0:T(4,128)S(1)}, f32[4,4,5]{2,1,0:T(4,128)}, u32[]{:S(2)}) %copy-start.2) | copy-done | bytes 344
  4.3 0.0 copy-start.3
  4.3 0.7 %copy-done.3 = f32[128,5]{0,1:T(8,128)S(1)} copy-done((f32[128,5]{0,1:T(8,128)S(1)}, f32[128,5]{0,1:T(8,128)}, u32[]{:S(2)}) %copy-start.3) | copy-done | bytes 2584
  5.0 42.8 %shard_map.86 = (f32[4,4,5]{2,1,0:T(4,128)S(1)}, f32[18,128]{1,0:T(8,128)S(1)}) custom-call(bf16[4,480,256]{2,1,0:T(8,128)(2,1)S(1)} %copy-done, bf16[2304,128]{1,0:T(8,128)(2,1)S(1)} %copy-done.1, f32[5,128]{1,0:T(8,128)S(1)} %bitcast.2, f32[4,4,5]{2,1,0:T(4,128)S(1)} %copy-done.2, s32[4]{0:T(128)S(1)} %copy-done.5, s32[4,8]{1,0:T(4,128)S(1)} %bitcast.3, ...), custom_call_target="tpu_custom_call" | custom-call | tf_op jit(solution)/shard_map/pallas_call | solution.py:325
  47.8 0.6 %copy.11 = f32[4,4,5]{2,1,0:T(4,128)} copy(f32[4,4,5]{2,1,0:T(4,128)S(1)} %get-tuple-element.4) | data formatting | bytes 640
  48.4 0.6 %copy.12 = f32[18,128]{1,0:T(8,128)} copy(f32[18,128]{1,0:T(8,128)S(1)} %get-tuple-element.5) | data formatting | bytes 18432
Async XLA Ops:
  0.6 0.7 %copy-start.4 = (s32[8,4]{0,1:T(4,128)S(1)}, s32[8,4]{0,1:T(4,128)}, u32[]{:S(2)}) copy-start(s32[8,4]{0,1:T(4,128)} %param.13) | copy-start | bytes 388
  0.6 0.7 %copy-start.5 = (s32[4]{0:T(128)S(1)}, s32[4]{0:T(128)}, u32[]{:S(2)}) copy-start(s32[4]{0:T(128)} %night.1) | copy-start | bytes 52
  0.7 0.7 %copy-start.6 = (f32[5]{0:T(128)S(1)}, f32[5]{0:T(128)}, u32[]{:S(2)}) copy-start(f32[5]{0:T(128)} %bias.1) | copy-start | bytes 64
  1.3 1.2 %copy-start = (bf16[4,480,256]{2,1,0:T(8,128)(2,1)S(1)}, bf16[4,480,256]{2,1,0:T(8,128)(2,1)}, u32[]{:S(2)}) copy-start(bf16[4,480,256]{2,1,0:T(8,128)(2,1)} %x.1) | copy-start | bytes 2949124
  2.5 1.1 %copy-start.1 = (bf16[2304,128]{1,0:T(8,128)(2,1)S(1)}, bf16[2304,128]{1,0:T(8,128)(2,1)}, u32[]{:S(2)}) copy-start(bf16[2304,128]{1,0:T(8,128)(2,1)} %w.1) | copy-start | bytes 1769476
  3.6 0.7 %copy-start.2 = (f32[4,4,5]{2,1,0:T(4,128)S(1)}, f32[4,4,5]{2,1,0:T(4,128)}, u32[]{:S(2)}) copy-start(f32[4,4,5]{2,1,0:T(4,128)} %tl.1) | copy-start | bytes 964
  4.3 0.7 %copy-start.3 = (f32[128,5]{0,1:T(8,128)S(1)}, f32[128,5]{0,1:T(8,128)}, u32[]{:S(2)}) copy-start(f32[128,5]{0,1:T(8,128)} %param.9) | copy-start | bytes 7684

commit v2 on v1

--- a/solution.py
+++ b/solution.py
@@ -14,15 +14,16 @@
 UNIT = 36
 WIDE = 2 * UNIT
 WIDE_PAD = 80
-SIXTEEN = False
+SIXTEEN = True
 
 
 def kernel(
-    x, w, cw, tl, night, labels, bias,
-    logits_out, grad_out,
+    x, w, cw_hbm, tl_hbm, night_hbm, labels_hbm, bias_hbm,
+    logits_hbm, grad_hbm,
+    cw, tl, night, labels, bias, logits_out, grad_out,
     xp, wv, y_taps, deriv, pooled, up, xt, grad,
     teach, logit, half_tx, half_rx, total, tx, rx, piece, tx2, rx2,
-    load_sem, halo_send, halo_recv, teach_send, teach_recv, logit_send, logit_recv,
+    small_sem, out_sem, load_sem, halo_send, halo_recv, teach_send, teach_recv, logit_send, logit_recv,
     half_send, half_recv, send1, recv1, send2, recv2,
 ):
     yy, tm, xx = lax.axis_index("inst"), lax.axis_index("tm"), lax.axis_index("filt")
@@ -37,13 +38,6 @@
 
     def arrived(dst, rsem):
         remote(dst, dst, rsem, rsem, (yy, tm, xx)).wait_recv()
-
-    loads = [pltpu.make_async_copy(w, wv, load_sem.at[4])]
-    loads += [
-        pltpu.make_async_copy(x.at[i], xp.at[i, pl.ds(PAD, 480)], load_sem.at[i]) for i in range(4)
-    ]
-    for c in loads:
-        c.start()
 
     barrier = pltpu.get_barrier_semaphore()
 
@@ -58,6 +52,17 @@
     for d in range(1, 4):
         greet((yy, tm, lax.rem(xx + d, nx)))
 
+    pairs = [(tl_hbm, tl), (night_hbm, night), (cw_hbm, cw), (labels_hbm, labels), (bias_hbm, bias)]
+    small = [pltpu.make_async_copy(src, dst, small_sem.at[i]) for i, (src, dst) in enumerate(pairs)]
+    loads = [pltpu.make_async_copy(w, wv, load_sem.at[4])]
+    loads += [
+        pltpu.make_async_copy(x.at[i], xp.at[i, pl.ds(PAD, 480)], load_sem.at[i]) for i in range(4)
+    ]
+    for c in small + loads:
+        c.start()
+
+    small[0].wait()
+    small[1].wait()
     row = lax.broadcasted_iota(i32, (16, 128), 0)
     lane = lax.broadcasted_iota(i32, (16, 128), 1)
     t5 = jnp.concatenate([tl[i] for i in range(4)], axis=0)
@@ -93,16 +98,26 @@
             if p < 4:
                 y_taps[i, 2 * p + 1, PAD : PAD + 480, :] = y[:, 128:]
 
-    loads[0].wait()
-    loads[1].wait()
-    forward(0)
+    def finish(i, epochs):
+        for e in epochs:
+            o = PAD - 4 + EPOCH * e
+            pre = y_taps[i, 0, pl.ds(o, EPOCH), :]
+            for k in range(1, 9):
+                pre = pre + y_taps[i, k, pl.ds(o + k, EPOCH), :]
+            ex = jnp.exp(jnp.minimum(pre, 0.0))
+            act = jnp.where(pre > 0, pre, ex - 1.0)
+            deriv[i, pl.ds(EPOCH * e, EPOCH), :] = ex
+            pooled[pl.ds(4 * i + e, 1), :] = jnp.sum(act, axis=0, keepdims=True) * (1.0 / EPOCH)
+
+    for c in loads:
+        c.wait()
     pl.semaphore_wait(barrier, 32)
 
     up_halo = remote(
-        x.at[:, pl.ds(480 - PAD, PAD)], xp.at[:, pl.ds(0, PAD)], halo_send.at[0], halo_recv.at[0], (yy, tm + 1, xx)
+        xp.at[:, pl.ds(480, PAD)], xp.at[:, pl.ds(0, PAD)], halo_send.at[0], halo_recv.at[0], (yy, tm + 1, xx)
     )
     down_halo = remote(
-        x.at[:, pl.ds(0, PAD)], xp.at[:, pl.ds(PAD + 480, PAD)], halo_send.at[1], halo_recv.at[1], (yy, tm - 1, xx)
+        xp.at[:, pl.ds(PAD, PAD)], xp.at[:, pl.ds(PAD + 480, PAD)], halo_send.at[1], halo_recv.at[1], (yy, tm - 1, xx)
     )
     pl.when(tm < 15)(up_halo.start)
     pl.when(tm > 0)(down_halo.start)
@@ -113,9 +128,9 @@
     for c in teach_copies:
         c.start()
 
-    for i in range(1, 4):
-        loads[1 + i].wait()
+    for i in range(4):
         forward(i)
+        finish(i, (1, 2))
 
     pl.when(tm > 0)(up_halo.wait_recv)
     pl.when(tm < 15)(down_halo.wait_recv)
@@ -130,16 +145,10 @@
                     y_taps[i, 2 * p + 1, r : r + PAD, :] = y[o : o + PAD, 128:]
 
     for i in range(4):
-        for e in range(4):
-            o = PAD - 4 + EPOCH * e
-            pre = y_taps[i, 0, pl.ds(o, EPOCH), :]
-            for k in range(1, 9):
-                pre = pre + y_taps[i, k, pl.ds(o + k, EPOCH), :]
-            ex = jnp.exp(jnp.minimum(pre, 0.0))
-            act = jnp.where(pre > 0, pre, ex - 1.0)
-            deriv[i, pl.ds(EPOCH * e, EPOCH), :] = ex
-            pooled[pl.ds(4 * i + e, 1), :] = jnp.sum(act, axis=0, keepdims=True) * (1.0 / EPOCH)
-
+        finish(i, (0, 3))
+
+    for c in small[2:]:
+        c.wait()
     cwt = cw[...]
     pool = pooled[...]
     part = jnp.zeros((16, 128), f32)
@@ -184,6 +193,8 @@
         logits = logits + jnp.where(lane == s, bias[s], 0.0)
     for i in range(4):
         logits_out[i] = logits[4 * i : 4 * i + 4, :5]
+    logits_copy = pltpu.make_async_copy(logits_out, logits_hbm, out_sem.at[0])
+    logits_copy.start()
     expo = jnp.where(lane < 5, jnp.exp(logits), 0.0)
     diff = expo / jnp.sum(expo, axis=1, keepdims=True) - target
     slope = jnp.zeros((16, 128), f32)
@@ -244,7 +255,7 @@
         else:
             for j in range(8 * part_at, 8 * part_at + 8):
                 tx[j] = total[j]
-        for d in range(1, 8):
+        for d in (4, 3, 5, 2, 6, 1, 7):
             if part_at == 0:
                 to, me = lax.rem(yy + d, ny), yy
                 dev = (to, tm, xx)
@@ -263,7 +274,7 @@
         base = 8 * part_at
         me = yy if part_at == 0 else zz
         acc = total[base + me]
-        for d in range(1, 8):
+        for d in (1, 7, 2, 6, 3, 5, 4):
             s = base + lax.rem(me + d, 8)
             arrived(rx.at[s], recv1.at[s])
             t = rx[s].astype(f32)
@@ -307,6 +318,8 @@
     for s in range(1, 8):
         out = out + rx2[s]
     grad_out[...] = out[:18] * (1.0 / 32)
+    grad_copy = pltpu.make_async_copy(grad_out, grad_hbm, out_sem.at[1])
+    grad_copy.start()
 
     pl.when(tm < 15)(up_halo.wait_send)
     pl.when(tm > 0)(down_halo.wait_send)
@@ -314,20 +327,27 @@
         c.wait_send()
     for c, mine in copies2:
         pl.when(jnp.logical_not(mine))(c.wait_send)
+    logits_copy.wait()
+    grad_copy.wait()
 
 
 def local(activations, conv_weight, class_weight, class_bias, teacher_logits, night_of, section_labels):
-    vm = pl.BlockSpec(memory_space=pltpu.VMEM)
-    sm = pl.BlockSpec(memory_space=pltpu.SMEM)
     hbm = pl.BlockSpec(memory_space=pltpu.HBM)
     wire, wire_rows = (i16, WIDE_PAD) if SIXTEEN else (f32, WIDE)
     dma = pltpu.SemaphoreType.DMA
     return pl.pallas_call(
         kernel,
         out_shape=(jax.ShapeDtypeStruct((4, 4, 5), f32), jax.ShapeDtypeStruct((18, 128), f32)),
-        in_specs=[hbm, hbm, vm, vm, sm, sm, sm],
-        out_specs=(vm, vm),
+        in_specs=[hbm] * 7,
+        out_specs=(hbm, hbm),
         scratch_shapes=[
+            pltpu.VMEM((5, 128), f32),
+            pltpu.VMEM((4, 4, 5), f32),
+            pltpu.SMEM((4,), i32),
+            pltpu.SMEM((4, 8), i32),
+            pltpu.SMEM((5,), f32),
+            pltpu.VMEM((4, 4, 5), f32),
+            pltpu.VMEM((18, 128), f32),
             pltpu.VMEM((4, 512, 256), bf16),
             pltpu.VMEM((2304, 128), bf16),
             pltpu.VMEM((4, 9, 512, 128), f32),
@@ -346,7 +366,7 @@
             pltpu.VMEM((2, WIDE_PAD, 128), f32),
             pltpu.VMEM((8, 24, 128), f32),
             pltpu.VMEM((8, 24, 128), f32),
-            dma((5,)),
+            dma((5,)), dma((2,)), dma((5,)),
             dma((2,)), dma((2,)),
             dma((7,)), dma((8,)),
             dma((3,)), dma((4,)),
@@ -355,7 +375,7 @@
             dma((8,)), dma((8,)),
         ],
         compiler_params=pltpu.CompilerParams(
-            collective_id=0, has_side_effects=True, vmem_limit_bytes=48 << 20
+            collective_id=0, has_side_effects=True, vmem_limit_bytes=63 << 20
         ),
     )(activations, conv_weight, class_weight.T, teacher_logits, night_of, section_labels.T, class_bias)
 

time: 49.3 us -> 39.6 us (0.80)
  Pallas kernels: 42.8 us -> 36.9 us
  local copies, waits for them, and re-layouts: 5.51 us -> 1.9 us
    pallas_call x1, Pallas kernels: 42.8 us -> 36.9 us  [local(): pl.pallas_call(kernel, out_shape=(jax.ShapeDtypeStruct((4, 4, 5), f32), j...]
    unnamed x16 -> x4, local copies, waits for them, and re-layouts: 5.51 us -> 1.9 us
where the time goes in v2:
time: 39.6 us; the launch traced here: 39.4 us
  Pallas kernels  36.9 us (93%)
  local copies, waits for them, and re-layouts  1.9 us (5%)
  between operations  0.65 us (2%)
    pallas_call x1, Pallas kernels, local(): pl.pallas_call(kernel, out_shape=(jax.ShapeDtypeStruct((4, 4, 5), f32), j...  36.9 us
    unnamed x4, local copies, waits for them, and re-layouts  1.9 us

profile of v2, /device:TPU:1, one launch (start us, length us, event | category | flops | bytes accessed | tf_op | source)
XLA Modules:
  0.0 39.4 jit_solution(11049712688755740826)
XLA Ops:
  0.6 36.9 %shard_map.86 = (f32[4,4,5]{2,1,0:T(4,128)}, f32[18,128]{1,0:T(8,128)}) custom-call(bf16[4,480,256]{2,1,0:T(8,128)(2,1)} %x.1, bf16[2304,128]{1,0:T(8,128)(2,1)} %w.1, f32[5,128]{1,0:T(8,128)} %bitcast.2, f32[4,4,5]{2,1,0:T(4,128)} %tl_hbm.1, s32[4]{0:T(128)} %night_hbm.1, s32[4,8]{1,0:T(4,128)} %bitcast.3, f32[5]{0:T(128)} %bias_hbm.1), custom_call_target="tpu_custom_call" | custom-call | tf_op jit(solution)/shard_map/pallas_call | solution.py:338
  37.5 0.0 copy-start
  37.5 1.3 %copy.11 = f32[4,4,5]{2,1,0:T(4,128)} copy(f32[4,4,5]{2,1,0:T(4,128)} %get-tuple-element.4) | data formatting | bytes 640
  38.8 0.0 copy-done
  38.8 0.6 %copy.12 = f32[18,128]{1,0:T(8,128)} copy(f32[18,128]{1,0:T(8,128)S(1)} %copy-done) | data formatting | bytes 18432
Async XLA Ops:
  37.5 1.3 %copy-start = (f32[18,128]{1,0:T(8,128)S(1)}, f32[18,128]{1,0:T(8,128)}, u32[]{:S(2)}) copy-start(f32[18,128]{1,0:T(8,128)} %get-tuple-element.5) | copy-start | bytes 27652

commit v3 on v2

v3 whole, which is shorter than its diff:
```python
import functools

import jax
import jax.numpy as jnp
from jax import lax
from jax.experimental import pallas as pl
from jax.experimental.pallas import tpu as pltpu
from jax.sharding import PartitionSpec as P

f32, bf16, i32, i16 = jnp.float32, jnp.bfloat16, jnp.int32, jnp.int16
MESH = pl.DeviceIdType.MESH
EPOCH = 120
PAD = 16
UNIT = 36
WIDE = 2 * UNIT
WIDE_PAD = 80
LONG = 1024
TN = False


def kernel(
    x, w, cw_hbm, tl_hbm, night_hbm, labels_hbm, bias_hbm,
    logits_out, grad_out,
    cw, tl, night, labels, bias,
    xc, wv, y_taps, deriv, pooled, up, xt, grad,
    teach, goal, logit, tx, rx, piece, tx2, rx2,
    small_sem, load_sem, halo_send, halo_recv, pair_send, pair_recv,
    teach_send, teach_recv, logit_send, logit_recv, send1, recv1, send2, recv2,
):
    yy, tm, xx = lax.axis_index("inst"), lax.axis_index("tm"), lax.axis_index("filt")
    zz, cc = tm // 2, tm % 2
    oc = 1 - cc
    ny, nz, nx = 8, 8, 4

    def remote(src, dst, ssem, rsem, dev):
        return pltpu.make_async_remote_copy(
            src_ref=src, dst_ref=dst, send_sem=ssem, recv_sem=rsem, device_id=dev, device_id_type=MESH
        )

    def arrived(dst, rsem):
        remote(dst, dst, rsem, rsem, (yy, tm, xx)).wait_recv()

    barrier = pltpu.get_barrier_semaphore()

    def greet(dev):
        pl.semaphore_signal(barrier, inc=1, device_id=dev, device_id_type=MESH)

    greet((yy, zz * 2 + oc, xx))
    for d in range(1, 8):
        for c in range(2):
            greet((yy, lax.rem(zz + d, nz) * 2 + c, xx))
            greet((lax.rem(yy + d, ny), zz * 2 + c, xx))
    for d in range(1, 4):
        for c in range(2):
            greet((yy, zz * 2 + c, lax.rem(xx + d, nx)))

    start = pl.multiple_of(480 * cc, 16)
    own = pl.ds(pl.multiple_of(PAD + 480 * cc, 16), 480)
    pairs = [(tl_hbm, tl), (night_hbm, night), (cw_hbm, cw), (labels_hbm, labels), (bias_hbm, bias)]
    small = [pltpu.make_async_copy(src, dst, small_sem.at[i]) for i, (src, dst) in enumerate(pairs)]
    loads = [pltpu.make_async_copy(w, wv, load_sem.at[4])]
    loads += [
        pltpu.make_async_copy(x.at[i], xc.at[i, own], load_sem.at[i]) for i in range(4)
    ]
    for c in small + loads:
        c.start()

    small[0].wait()
    small[1].wait()
    row = lax.broadcasted_iota(i32, (16, 128), 0)
    lane = lax.broadcasted_iota(i32, (16, 128), 1)
    t5 = jnp.concatenate([tl[i] for i in range(4)], axis=0)
    t5 = jnp.exp(t5 - jnp.max(t5, axis=1, keepdims=True))
    t5 = t5 / jnp.sum(t5, axis=1, keepdims=True)
    tile = jnp.zeros((16, 128), f32)
    for s in range(5):
        tile = jnp.where(lane == s, t5[:, s : s + 1], tile)
    for i in range(4):
        tile = jnp.where((lane == 8) & (row // 4 == i), night[i].astype(f32), tile)
    tile = jnp.where(lane == 9, 1.0, tile)
    teach[yy] = tile[0:8] + pltpu.roll(tile[8:16], 16, 1)

    @pl.when(zz == 0)
    def _():
        for i in range(4):
            xc[i, 0:PAD, :] = jnp.zeros((PAD, 256), bf16)

    @pl.when(zz == nz - 1)
    def _():
        for i in range(4):
            xc[i, PAD + 960 : 2 * PAD + 960, :] = jnp.zeros((PAD, 256), bf16)

    for i in range(4):
        xc[i, 2 * PAD + 960 :, :] = jnp.zeros((LONG - 2 * PAD - 960, 256), bf16)
        up[i, 0:24, :] = jnp.zeros((24, 128), f32)
        up[i, 984:, :] = jnp.zeros((56, 128), f32)

    def weights(p):
        if p == 4:
            return wv[pl.ds(2048, 256), :]
        return jnp.concatenate([wv[pl.ds(512 * p, 256), :], wv[pl.ds(512 * p + 256, 256), :]], axis=1)

    def forward(i):
        for p in range(5):
            y = jnp.dot(xc[i, own, :], weights(p), preferred_element_type=f32)
            y_taps[i, 2 * p, PAD : PAD + 480, :] = y[:, :128]
            if p < 4:
                y_taps[i, 2 * p + 1, PAD : PAD + 480, :] = y[:, 128:]

    def finish(i, epochs):
        for e in epochs:
            o = PAD - 4 + EPOCH * e
            pre = y_taps[i, 0, pl.ds(o, EPOCH), :]
            for k in range(1, 9):
                pre = pre + y_taps[i, k, pl.ds(o + k, EPOCH), :]
            ex = jnp.exp(jnp.minimum(pre, 0.0))
            act = jnp.where(pre > 0, pre, ex - 1.0)
            deriv[i, pl.ds(pl.multiple_of(start + EPOCH * e, 8), EPOCH), :] = ex
            pooled[pl.ds(4 * i + e, 1), :] = jnp.sum(act, axis=0, keepdims=True) * (1.0 / EPOCH)

    for c in loads:
        c.wait()
    pl.semaphore_wait(barrier, 35)

    partner = (yy, zz * 2 + oc, xx)
    pair_copies = []

    def to_partner(ref, rows):
        k = len(pair_copies)
        c = remote(ref.at[:, rows], ref.at[:, rows], pair_send.at[k], pair_recv.at[k], partner)
        c.start()
        pair_copies.append(c)

    halo_src = pl.ds(pl.multiple_of(PAD + 944 * cc, 16), PAD)
    halo_dst = pl.ds(pl.multiple_of((PAD + 960) * oc, 16), PAD)
    has_next = jnp.where(cc == 0, zz > 0, zz < nz - 1)
    halo_copies = [
        remote(
            xc.at[:, halo_src], xc.at[:, halo_dst], halo_send.at[c], halo_recv.at[oc],
            (yy, (zz - 1 + 2 * cc) * 2 + c, xx),
        )
        for c in range(2)
    ]

    @pl.when(has_next)
    def _():
        for c in halo_copies:
            c.start()

    teach_copies = [
        remote(teach.at[yy], teach.at[yy], teach_send.at[d - 1], teach_recv.at[yy], (lax.rem(yy + d, ny), tm, xx))
        for d in (4, 3, 5, 2, 6, 1, 7)
    ]
    for c in teach_copies:
        c.start()
    to_partner(xc, pl.ds(pl.multiple_of(480 + 16 * cc, 16), PAD))

    for i in range(4):
        forward(i)
        finish(i, (1, 2))

    to_partner(xc, pl.ds(pl.multiple_of(PAD + 496 * cc, 16), 464))
    to_partner(deriv, pl.ds(pl.multiple_of(start + EPOCH, 8), 2 * EPOCH))
    pair_copies[0].wait_recv()

    @pl.when(zz > 0)
    def _():
        arrived(xc.at[:, pl.ds(0, PAD)], halo_recv.at[0])

    @pl.when(zz < nz - 1)
    def _():
        arrived(xc.at[:, pl.ds(PAD + 960, PAD)], halo_recv.at[1])

    ends = [pl.ds(start, PAD), pl.ds(pl.multiple_of(start + PAD + 480, 16), PAD)]
    xh = jnp.concatenate([xc[i, r, :] for i in range(4) for r in ends], axis=0)
    for p in range(5):
        y = jnp.dot(xh, weights(p), preferred_element_type=f32)
        for i in range(4):
            for h, r in enumerate((0, PAD + 480)):
                o = (2 * i + h) * PAD
                y_taps[i, 2 * p, r : r + PAD, :] = y[o : o + PAD, :128]
                if p < 4:
                    y_taps[i, 2 * p + 1, r : r + PAD, :] = y[o : o + PAD, 128:]

    for i in range(4):
        finish(i, (0, 3))

    for c in small[2:]:
        c.wait()
    cwt = cw[...]
    pool = pooled[...]
    part = jnp.zeros((8, 128), f32)
    for s in range(5):
        t = jnp.sum(pool * cwt[s : s + 1, :], axis=1, keepdims=True)
        part = jnp.where(lane[0:8] == s, t[0:8], part)
        part = jnp.where(lane[0:8] == 16 + s, t[8:16], part)
    logit[cc, xx] = part
    logit_copies = []
    for d in (2, 1, 3, 0):
        for c in range(2):
            if d:
                dev = (yy, zz * 2 + c, lax.rem(xx + d, nx))
            elif c == 0:
                dev = partner
            else:
                continue
            k = len(logit_copies)
            logit_copies.append(
                remote(logit.at[cc, xx], logit.at[cc, xx], logit_send.at[k], logit_recv.at[cc, xx], dev)
            )
    for c in logit_copies:
        c.start()

    to_partner(deriv, pl.ds(start, EPOCH))
    to_partner(deriv, pl.ds(pl.multiple_of(start + 3 * EPOCH, 8), EPOCH))

    pair_copies[1].wait_recv()
    for i in range(4):
        xt[i] = xc[i].T
    for d in range(1, 8):
        s = lax.rem(yy + d, ny)
        arrived(teach.at[s], teach_recv.at[s])
    nights = [night[i].astype(f32) for i in range(4)]
    lane8 = lane[0:8]
    sums = [jnp.zeros((8, 128), f32) for _ in range(4)]
    for j in range(8):
        t = teach[j]
        of = jnp.where(lane8 < 16, t[:, 8:9], t[:, 24:25])
        for i in range(4):
            sums[i] = sums[i] + jnp.where(of == nights[i], t, 0.0)
    soft = []
    for i in range(4):
        s = sums[i] + pltpu.roll(sums[i], 112, 1)
        s = s[0:4] + s[4:8]
        soft.append(s / s[:, 9:10])
    soft = jnp.concatenate(soft, axis=0)
    label = jnp.zeros((16, 128), i32)
    for i in range(4):
        for e in range(4):
            label = jnp.where(row == 4 * i + e, labels[e, night[i]], label)
    goal[cc] = 0.5 * soft + 0.5 * (lane == label).astype(f32)
    goal_copy = remote(goal.at[cc], goal.at[cc], pair_send.at[5], pair_recv.at[5], partner)
    goal_copy.start()

    for d in range(1, 4):
        s = lax.rem(xx + d, nx)
        for c in range(2):
            arrived(logit.at[c, s], logit_recv.at[c, s])
    arrived(logit.at[oc, xx], logit_recv.at[oc, xx])
    goal_copy.wait_recv()
    shift = jnp.zeros((16, 128), f32)
    for s in range(5):
        shift = shift + jnp.where(lane == s, bias[s], 0.0)
    slopes, both = [], []
    for b in range(2):
        logits = logit[b, 0] + logit[b, 1] + logit[b, 2] + logit[b, 3]
        logits = jnp.concatenate([logits, pltpu.roll(logits, 112, 1)], axis=0) + shift
        both.append(logits)
        expo = jnp.where(lane < 5, jnp.exp(logits), 0.0)
        diff = expo / jnp.sum(expo, axis=1, keepdims=True) - goal[b]
        slope = jnp.zeros((16, 128), f32)
        for s in range(5):
            slope = slope + diff[:, s : s + 1] * cwt[s : s + 1, :]
        slopes.append(slope)
    logits = jnp.where(cc == 0, both[0], both[1])
    for i in range(4):
        logits_out[i] = logits[4 * i : 4 * i + 4, :5]

    for c in pair_copies[2:]:
        c.wait_recv()
    for i in range(4):
        for b in range(2):
            for e in range(4):
                o = 480 * b + EPOCH * e
                up[i, pl.ds(24 + o, EPOCH), :] = (
                    deriv[i, pl.ds(o, EPOCH), :] * slopes[b][4 * i + e : 4 * i + e + 1, :]
                )

    def backward(taps, channels, at):
        acc = None
        for i in range(4):
            us = [up[i, pl.ds(12 - k, LONG), :].astype(bf16) for k in taps]
            u = us[0] if len(us) == 1 else jnp.concatenate(us, axis=1)
            g = jnp.dot(xt[i, channels, :], u, preferred_element_type=f32)
            acc = g if acc is None else acc + g
        for n in range(len(taps)):
            grad[pl.ds(at + acc.shape[0] * n, acc.shape[0]), :] = acc[:, 128 * n : 128 * n + 128]

    @pl.when(cc == 0)
    def _():
        backward((0, 1), slice(None), 0)
        backward((2, 3), slice(None), 512)
        backward((4,), slice(0, 128), 1024)

    @pl.when(cc == 1)
    def _():
        backward((4,), slice(128, 256), 0)
        backward((5, 6), slice(None), 128)
        backward((7, 8), slice(None), 640)

    def rows_of(j, h):
        if j < 8:
            y, z = j // 2, j // 2 % 2 + 4 * (j % 2) + 2 * h
        else:
            y, z = 1 - j % 2 + 2 * h, j - 8
        return pl.ds(288 * y + UNIT * z, UNIT)

    holder1 = yy // 4 == cc
    copies1 = []
    for part_at in range(2):
        base = 8 * part_at
        top = jnp.max(jnp.abs(grad[...]), axis=0, keepdims=True) if part_at == 0 else top
        if part_at == 0:
            power = jnp.ceil(jnp.log2(jnp.maximum(top, 1e-30)) + 0.01)
            factor = jnp.exp2(15.0 - power)
            power = jnp.broadcast_to(power, (WIDE_PAD - WIDE, 128))
        for j in range(base, base + 8):
            t = jnp.concatenate([grad[rows_of(j, h), :] for h in range(2)], axis=0)
            q = jnp.concatenate([jnp.round(t * factor), power], axis=0)
            tx[j] = q.astype(i32).astype(i16)
        if part_at == 0:
            for m, (near, far) in enumerate(((2, 0), (3, 1), (1, 3), (0, 2))):
                j = lax.rem(yy + jnp.where(holder1, near, far), 4)
                for h in range(2):
                    mine = (yy == 4 * cc + j) & (cc == h)
                    c = remote(
                        tx.at[2 * j + h], rx.at[yy], send1.at[2 * m + h], recv1.at[yy], (4 * cc + j, zz * 2 + h, xx)
                    )
                    copies1.append((c, mine))
                    pl.when(jnp.logical_not(mine))(c.start)

            @pl.when(holder1)
            def _():
                rx[yy] = tx[2 * lax.rem(yy, 4) + cc]

        else:
            rx[8 + zz] = tx[8 + zz]
            for d in (4, 3, 5, 2, 6, 1, 7):
                to = lax.rem(zz + d, nz)
                c = remote(
                    tx.at[8 + to], rx.at[8 + zz], send1.at[8 + d], recv1.at[8 + zz], (yy, to * 2 + cc, xx)
                )
                c.start()
                copies1.append((c, None))

    copies2 = []
    for part_at in range(2):
        base = 8 * part_at
        me = yy if part_at == 0 else zz
        if part_at == 0:
            for s in range(8):
                @pl.when(jnp.logical_not(holder1 & (yy == s)))
                def _():
                    arrived(rx.at[s], recv1.at[s])
        else:
            for d in (1, 7, 2, 6, 3, 5, 4):
                s = base + lax.rem(me + d, 8)
                arrived(rx.at[s], recv1.at[s])
        acc = jnp.zeros((WIDE, 128), f32)
        for s in range(base, base + 8):
            t = rx[s].astype(f32)
            acc = acc + t[:WIDE] * jnp.exp2(t[WIDE : WIDE + 1] - 15.0)
        piece[part_at, 0:WIDE, :] = acc
        piece[part_at, WIDE:, :] = jnp.zeros((WIDE_PAD - WIDE, 128), f32)
        for m in range(4):
            tx2[4 * part_at + m] = piece[part_at, pl.ds(18 * m, 24), :]
        for m in range(4):
            h, c = m // 2, m % 2
            slot = 4 * part_at + m
            if part_at == 0:
                to, own = yy % 2 + 4 * cc + 2 * h, zz
                dev = (yy, to * 2 + c, xx)
                mine = (to == zz) & (cc == c)
            else:
                to, own = 4 * cc + 1 - zz % 2 + 2 * h, yy
                dev = (to, zz * 2 + c, xx)
                mine = (to == yy) & (cc == c)
            copy = remote(tx2.at[slot], rx2.at[own], send2.at[slot], recv2.at[own], dev)
            copies2.append((copy, mine))

            @pl.when(mine)
            def _():
                rx2[own] = tx2[slot]

            @pl.when(jnp.logical_not(mine))
            def _():
                copy.start()

    even = (yy + zz) % 2 == 0
    holder = jnp.where(even, zz // 4, yy // 4)
    place = jnp.where(even, zz, yy)
    for s in range(8):
        @pl.when(jnp.logical_not((place == s) & (holder == cc)))
        def _():
            arrived(rx2.at[s], recv2.at[s])
    out = rx2[0]
    for s in range(1, 8):
        out = out + rx2[s]
    grad_out[...] = out[:18] * (1.0 / 32)

    @pl.when(has_next)
    def _():
        for c in halo_copies:
            c.wait_send()

    for c in pair_copies + [goal_copy] + teach_copies + logit_copies:
        c.wait_send()
    for c, mine in copies1 + copies2:
        if mine is None:
            c.wait_send()
        else:
            pl.when(jnp.logical_not(mine))(c.wait_send)


def local(activations, conv_weight, class_weight, class_bias, teacher_logits, night_of, section_labels):
    hbm = pl.BlockSpec(memory_space=pltpu.HBM)
    vm = pl.BlockSpec(memory_space=pltpu.VMEM)
    dma = pltpu.SemaphoreType.DMA
    return pl.pallas_call(
        kernel,
        out_shape=(pltpu.VMEM((4, 4, 5), f32), pltpu.VMEM((18, 128), f32)),
        in_specs=[hbm] * 7,
        out_specs=(vm, vm),
        scratch_shapes=[
            pltpu.VMEM((5, 128), f32),
            pltpu.VMEM((4, 4, 5), f32),
            pltpu.SMEM((4,), i32),
            pltpu.SMEM((4, 8), i32),
            pltpu.SMEM((5,), f32),
            pltpu.VMEM((4, LONG, 256), bf16),
            pltpu.VMEM((2304, 128), bf16),
            pltpu.VMEM((4, 9, 512, 128), f32),
            pltpu.VMEM((4, 960, 128), f32),
            pltpu.VMEM((16, 128), f32),
            pltpu.VMEM((4, LONG + 16, 128), f32),
            pltpu.VMEM((4, 256, LONG), bf16),
            pltpu.VMEM((1152, 128), f32),
            pltpu.VMEM((8, 8, 128), f32),
            pltpu.VMEM((2, 16, 128), f32),
            pltpu.VMEM((2, 4, 8, 128), f32),
            pltpu.VMEM((16, WIDE_PAD, 128), i16),
            pltpu.VMEM((16, WIDE_PAD, 128), i16),
            pltpu.VMEM((2, WIDE_PAD, 128), f32),
            pltpu.VMEM((8, 24, 128), f32),
            pltpu.VMEM((8, 24, 128), f32),
            dma((5,)), dma((5,)),
            dma((2,)), dma((2,)),
            dma((6,)), dma((6,)),
            dma((7,)), dma((8,)),
            dma((7,)), dma((2, 4)),
            dma((16,)), dma((16,)),
            dma((8,)), dma((8,)),
        ],
        compiler_params=pltpu.CompilerParams(
            collective_id=0, has_side_effects=True, vmem_limit_bytes=63 << 20
        ),
    )(activations, conv_weight, class_weight.T, teacher_logits, night_of, section_labels.T, class_bias)


def solution(mesh):
    in_specs = (
        P("inst", "tm", None),
        P(None, "filt"),
        P("filt", None),
        P(),
        P("inst", "tm", None),
        P("inst"),
        P(None, "tm"),
    )
    out_specs = (P("inst", "tm", None), P(("inst", "tm"), "filt"))
    return jax.shard_map(local, mesh=mesh, in_specs=in_specs, out_specs=out_specs, check_vma=False)
```

time: 39.6 us -> 39 us (0.985)
  local copies, waits for them, and re-layouts: 1.9 us -> 1.2 us
    unnamed x4 -> x2, local copies, waits for them, and re-layouts: 1.9 us -> 1.2 us
where the time goes in v3:
time: 39 us; the launch traced here: 38.9 us
  Pallas kernels  37.1 us (95%)
  local copies, waits for them, and re-layouts  1.2 us (3%)
  between operations  0.64 us (2%)
    pallas_call x1, Pallas kernels, local(): pl.pallas_call(kernel, out_shape=(pltpu.VMEM((4, 4, 5), f32), pltpu.VMEM(...  37.1 us
    unnamed x2, local copies, waits for them, and re-layouts  1.2 us

profile of v3, /device:TPU:1, one launch (start us, length us, event | category | flops | bytes accessed | tf_op | source)
XLA Modules:
  0.0 38.9 jit_solution(16049730528346183993)
XLA Ops:
  0.6 37.1 %shard_map.86 = (f32[4,4,5]{2,1,0:T(4,128)S(1)}, f32[18,128]{1,0:T(8,128)S(1)}) custom-call(bf16[4,480,256]{2,1,0:T(8,128)(2,1)} %x.1, bf16[2304,128]{1,0:T(8,128)(2,1)} %w.1, f32[5,128]{1,0:T(8,128)} %bitcast.2, f32[4,4,5]{2,1,0:T(4,128)} %tl_hbm.1, s32[4]{0:T(128)} %night_hbm.1, s32[4,8]{1,0:T(4,128)} %bitcast.3, f32[5]{0:T(128)} %bias_hbm.1), custom_call_target="tpu_custom_call" | custom-call | tf_op jit(solution)/shard_map/pallas_call | solution.py:419
  37.7 0.6 %copy.11 = f32[4,4,5]{2,1,0:T(4,128)} copy(f32[4,4,5]{2,1,0:T(4,128)S(1)} %get-tuple-element.2) | data formatting | bytes 640
  38.3 0.6 %copy.12 = f32[18,128]{1,0:T(8,128)} copy(f32[18,128]{1,0:T(8,128)S(1)} %get-tuple-element.3) | data formatting | bytes 18432

commit v4 on v3

--- a/solution.py
+++ b/solution.py
@@ -13,7 +13,6 @@
 PAD = 16
 UNIT = 36
 WIDE = 2 * UNIT
-WIDE_PAD = 80
 LONG = 1024
 TN = False
 
@@ -45,14 +44,24 @@
     def greet(dev):
         pl.semaphore_signal(barrier, inc=1, device_id=dev, device_id_type=MESH)
 
-    greet((yy, zz * 2 + oc, xx))
-    for d in range(1, 8):
+    def greet_z(d):
         for c in range(2):
             greet((yy, lax.rem(zz + d, nz) * 2 + c, xx))
+
+    def greet_y(d):
+        for c in range(2):
             greet((lax.rem(yy + d, ny), zz * 2 + c, xx))
+
+    greet_z(7)
+    greet_z(1)
+    greet((yy, zz * 2 + oc, xx))
     for d in range(1, 4):
         for c in range(2):
             greet((yy, zz * 2 + c, lax.rem(xx + d, nx)))
+    for d in (1, 7, 2, 6, 3, 5, 4):
+        greet_y(d)
+    for d in (6, 2, 5, 3, 4):
+        greet_z(d)
 
     start = pl.multiple_of(480 * cc, 16)
     own = pl.ds(pl.multiple_of(PAD + 480 * cc, 16), 480)
@@ -147,9 +156,10 @@
         for c in halo_copies:
             c.start()
 
+    nearby = (2, 6, 1, 7)
     teach_copies = [
-        remote(teach.at[yy], teach.at[yy], teach_send.at[d - 1], teach_recv.at[yy], (lax.rem(yy + d, ny), tm, xx))
-        for d in (4, 3, 5, 2, 6, 1, 7)
+        remote(teach.at[yy], teach.at[yy], teach_send.at[k], teach_recv.at[yy], (lax.rem(yy + d, ny), tm, xx))
+        for k, d in enumerate(nearby)
     ]
     for c in teach_copies:
         c.start()
@@ -217,14 +227,14 @@
     pair_copies[1].wait_recv()
     for i in range(4):
         xt[i] = xc[i].T
-    for d in range(1, 8):
+    for d in nearby:
         s = lax.rem(yy + d, ny)
         arrived(teach.at[s], teach_recv.at[s])
     nights = [night[i].astype(f32) for i in range(4)]
     lane8 = lane[0:8]
     sums = [jnp.zeros((8, 128), f32) for _ in range(4)]
-    for j in range(8):
-        t = teach[j]
+    for d in (0, *nearby):
+        t = teach[lax.rem(yy + d, ny)]
         of = jnp.where(lane8 < 16, t[:, 8:9], t[:, 24:25])
         for i in range(4):
             sums[i] = sums[i] + jnp.where(of == nights[i], t, 0.0)
@@ -298,96 +308,97 @@
         backward((5, 6), slice(None), 128)
         backward((7, 8), slice(None), 640)
 
-    def rows_of(j, h):
-        if j < 8:
-            y, z = j // 2, j // 2 % 2 + 4 * (j % 2) + 2 * h
-        else:
-            y, z = 1 - j % 2 + 2 * h, j - 8
-        return pl.ds(288 * y + UNIT * z, UNIT)
-
-    holder1 = yy // 4 == cc
-    copies1 = []
-    for part_at in range(2):
-        base = 8 * part_at
-        top = jnp.max(jnp.abs(grad[...]), axis=0, keepdims=True) if part_at == 0 else top
-        if part_at == 0:
-            power = jnp.ceil(jnp.log2(jnp.maximum(top, 1e-30)) + 0.01)
-            factor = jnp.exp2(15.0 - power)
-            power = jnp.broadcast_to(power, (WIDE_PAD - WIDE, 128))
-        for j in range(base, base + 8):
-            t = jnp.concatenate([grad[rows_of(j, h), :] for h in range(2)], axis=0)
-            q = jnp.concatenate([jnp.round(t * factor), power], axis=0)
-            tx[j] = q.astype(i32).astype(i16)
-        if part_at == 0:
-            for m, (near, far) in enumerate(((2, 0), (3, 1), (1, 3), (0, 2))):
-                j = lax.rem(yy + jnp.where(holder1, near, far), 4)
-                for h in range(2):
-                    mine = (yy == 4 * cc + j) & (cc == h)
-                    c = remote(
-                        tx.at[2 * j + h], rx.at[yy], send1.at[2 * m + h], recv1.at[yy], (4 * cc + j, zz * 2 + h, xx)
-                    )
-                    copies1.append((c, mine))
-                    pl.when(jnp.logical_not(mine))(c.start)
-
-            @pl.when(holder1)
-            def _():
-                rx[yy] = tx[2 * lax.rem(yy, 4) + cc]
-
-        else:
-            rx[8 + zz] = tx[8 + zz]
-            for d in (4, 3, 5, 2, 6, 1, 7):
-                to = lax.rem(zz + d, nz)
-                c = remote(
-                    tx.at[8 + to], rx.at[8 + zz], send1.at[8 + d], recv1.at[8 + zz], (yy, to * 2 + cc, xx)
-                )
-                c.start()
-                copies1.append((c, None))
-
-    copies2 = []
-    for part_at in range(2):
-        base = 8 * part_at
-        me = yy if part_at == 0 else zz
-        if part_at == 0:
-            for s in range(8):
-                @pl.when(jnp.logical_not(holder1 & (yy == s)))
+    power = jnp.ceil(jnp.log2(jnp.maximum(jnp.max(jnp.abs(grad[...]), axis=0, keepdims=True), 1e-30)) + 0.01)
+    factor = jnp.exp2(15.0 - power)
+    power = jnp.broadcast_to(power, (8, 128))
+
+    def code(slot, units):
+        t = jnp.concatenate([grad[pl.ds(288 * y + UNIT * z, UNIT), :] for y, z in units], axis=0)
+        tx[slot] = jnp.concatenate([jnp.round(t * factor), power], axis=0).astype(i32).astype(i16)
+
+    half_y, half_z = yy // 4 == cc, zz // 4
+    copies = []
+
+    def send(copy, sent):
+        copies.append((copy, sent))
+        pl.when(sent)(copy.start)
+
+    far_first = ((2, 0), (3, 1), (1, 3), (0, 2))
+    for h in range(2):
+        for j in range(4):
+            code(2 * j + h, [(j, j % 2 + 4 * h), (j, j % 2 + 4 * h + 2)])
+        for m, (near, far) in enumerate(far_first):
+            j = lax.rem(yy + jnp.where(half_y, near, far), 4)
+            dev = (4 * cc + j, zz * 2 + h, xx)
+            send(
+                remote(tx.at[2 * j + h], rx.at[yy], send1.at[4 * h + m], recv1.at[yy], dev),
+                jnp.logical_not((yy == 4 * cc + j) & (cc == h)),
+            )
+        for z in range(4 * h, 4 * h + 4):
+            code(8 + z, [(1 - z % 2, z), (3 - z % 2, z)])
+        for m, (near, far) in enumerate(far_first):
+            z = 4 * h + lax.rem(zz + jnp.where(half_z == h, near, far), 4)
+            dev = (yy, z * 2 + cc, xx)
+            send(
+                remote(tx.at[8 + z], rx.at[8 + zz], send1.at[8 + 4 * h + m], recv1.at[8 + zz], dev),
+                zz != z,
+            )
+
+    @pl.when(half_y)
+    def _():
+        rx[yy] = tx[2 * lax.rem(yy, 4) + cc]
+
+    rx[8 + zz] = tx[8 + zz]
+
+    handed = []
+    for k in range(2):
+        for m in range(4):
+            if k == 0:
+                own, dev = zz, (yy, (yy % 2 + 4 * cc + 2 * (m // 2)) * 2 + m % 2, xx)
+            else:
+                own, dev = yy, (4 * cc + 1 - zz % 2 + 2 * (m // 2), zz * 2 + m % 2, xx)
+            slot = 4 * k + m
+            copy = remote(tx2.at[slot], rx2.at[own], send2.at[slot], recv2.at[own], dev)
+            handed.append((copy, (dev[0] != yy) | (dev[1] != tm), own))
+
+    def hand_out(k):
+        acc = jnp.zeros((WIDE, 128), f32)
+        for s in range(8):
+            if k == 0:
+                @pl.when(jnp.logical_not(half_y & (yy == s)))
                 def _():
                     arrived(rx.at[s], recv1.at[s])
-        else:
-            for d in (1, 7, 2, 6, 3, 5, 4):
-                s = base + lax.rem(me + d, 8)
-                arrived(rx.at[s], recv1.at[s])
-        acc = jnp.zeros((WIDE, 128), f32)
-        for s in range(base, base + 8):
+            else:
+                @pl.when(zz != s)
+                def _():
+                    arrived(rx.at[8 + s], recv1.at[8 + s])
+        for s in range(8 * k, 8 * k + 8):
             t = rx[s].astype(f32)
             acc = acc + t[:WIDE] * jnp.exp2(t[WIDE : WIDE + 1] - 15.0)
-        piece[part_at, 0:WIDE, :] = acc
-        piece[part_at, WIDE:, :] = jnp.zeros((WIDE_PAD - WIDE, 128), f32)
-        for m in range(4):
-            tx2[4 * part_at + m] = piece[part_at, pl.ds(18 * m, 24), :]
-        for m in range(4):
-            h, c = m // 2, m % 2
-            slot = 4 * part_at + m
-            if part_at == 0:
-                to, own = yy % 2 + 4 * cc + 2 * h, zz
-                dev = (yy, to * 2 + c, xx)
-                mine = (to == zz) & (cc == c)
-            else:
-                to, own = 4 * cc + 1 - zz % 2 + 2 * h, yy
-                dev = (to, zz * 2 + c, xx)
-                mine = (to == yy) & (cc == c)
-            copy = remote(tx2.at[slot], rx2.at[own], send2.at[slot], recv2.at[own], dev)
-            copies2.append((copy, mine))
-
-            @pl.when(mine)
+        piece[0:WIDE, :] = acc
+        piece[WIDE:, :] = jnp.zeros((8, 128), f32)
+        for slot in range(4 * k, 4 * k + 4):
+            copy, sent, own = handed[slot]
+            tx2[slot] = piece[pl.ds(18 * (slot % 4), 24), :]
+            pl.when(sent)(copy.start)
+
+            @pl.when(jnp.logical_not(sent))
             def _():
                 rx2[own] = tx2[slot]
 
-            @pl.when(jnp.logical_not(mine))
-            def _():
-                copy.start()
-
+    @pl.when(cc == 0)
+    def _():
+        hand_out(0)
+        hand_out(1)
+
+    @pl.when(cc == 1)
+    def _():
+        hand_out(1)
+        hand_out(0)
+
+    copies += [(copy, sent) for copy, sent, _ in handed]
     even = (yy + zz) % 2 == 0
-    holder = jnp.where(even, zz // 4, yy // 4)
+    holder = jnp.where(even, half_z, yy // 4)
     place = jnp.where(even, zz, yy)
     for s in range(8):
         @pl.when(jnp.logical_not((place == s) & (holder == cc)))
@@ -405,11 +416,8 @@
 
     for c in pair_copies + [goal_copy] + teach_copies + logit_copies:
         c.wait_send()
-    for c, mine in copies1 + copies2:
-        if mine is None:
-            c.wait_send()
-        else:
-            pl.when(jnp.logical_not(mine))(c.wait_send)
+    for c, sent in copies:
+        pl.when(sent)(c.wait_send)
 
 
 def local(activations, conv_weight, class_weight, class_bias, teacher_logits, night_of, section_labels):
@@ -438,15 +446,15 @@
             pltpu.VMEM((8, 8, 128), f32),
             pltpu.VMEM((2, 16, 128), f32),
             pltpu.VMEM((2, 4, 8, 128), f32),
-            pltpu.VMEM((16, WIDE_PAD, 128), i16),
-            pltpu.VMEM((16, WIDE_PAD, 128), i16),
-            pltpu.VMEM((2, WIDE_PAD, 128), f32),
+            pltpu.VMEM((16, WIDE + 8, 128), i16),
+            pltpu.VMEM((16, WIDE + 8, 128), i16),
+            pltpu.VMEM((WIDE + 8, 128), f32),
             pltpu.VMEM((8, 24, 128), f32),
             pltpu.VMEM((8, 24, 128), f32),
             dma((5,)), dma((5,)),
             dma((2,)), dma((2,)),
             dma((6,)), dma((6,)),
-            dma((7,)), dma((8,)),
+            dma((4,)), dma((8,)),
             dma((7,)), dma((2, 4)),
             dma((16,)), dma((16,)),
             dma((8,)), dma((8,)),

time: 39 us -> 38.3 us (0.982)
  Pallas kernels: 37.1 us -> 36.3 us
    pallas_call x1, Pallas kernels: 37.1 us -> 36.3 us  [local(): pl.pallas_call(kernel, out_shape=(pltpu.VMEM((4, 4, 5), f32), pltpu.VMEM(...]
where the time goes in v4:
time: 38.3 us; the launch traced here: 38.1 us
  Pallas kernels  36.3 us (95%)
  local copies, waits for them, and re-layouts  1.2 us (3%)
  between operations  0.64 us (2%)
    pallas_call x1, Pallas kernels, local(): pl.pallas_call(kernel, out_shape=(pltpu.VMEM((4, 4, 5), f32), pltpu.VMEM(...  36.3 us
    unnamed x2, local copies, waits for them, and re-layouts  1.2 us

profile of v4, /device:TPU:1, one launch (start us, length us, event | category | flops | bytes accessed | tf_op | source)
XLA Modules:
  0.0 38.1 jit_solution(3147883418108518451)
XLA Ops:
  0.6 36.3 %shard_map.86 = (f32[4,4,5]{2,1,0:T(4,128)S(1)}, f32[18,128]{1,0:T(8,128)S(1)}) custom-call(bf16[4,480,256]{2,1,0:T(8,128)(2,1)} %x.1, bf16[2304,128]{1,0:T(8,128)(2,1)} %w.1, f32[5,128]{1,0:T(8,128)} %bitcast.2, f32[4,4,5]{2,1,0:T(4,128)} %tl_hbm.1, s32[4]{0:T(128)} %night_hbm.1, s32[4,8]{1,0:T(4,128)} %bitcast.3, f32[5]{0:T(128)} %bias_hbm.1), custom_call_target="tpu_custom_call" | custom-call | tf_op jit(solution)/shard_map/pallas_call | solution.py:427
  36.9 0.6 %copy.11 = f32[4,4,5]{2,1,0:T(4,128)} copy(f32[4,4,5]{2,1,0:T(4,128)S(1)} %get-tuple-element.2) | data formatting | bytes 640
  37.5 0.6 %copy.12 = f32[18,128]{1,0:T(8,128)} copy(f32[18,128]{1,0:T(8,128)S(1)} %get-tuple-element.3) | data formatting | bytes 18432

commit v5 on v4

--- a/solution.py
+++ b/solution.py
@@ -24,7 +24,7 @@
     xc, wv, y_taps, deriv, pooled, up, xt, grad,
     teach, goal, logit, tx, rx, piece, tx2, rx2,
     small_sem, load_sem, halo_send, halo_recv, pair_send, pair_recv,
-    teach_send, teach_recv, logit_send, logit_recv, send1, recv1, send2, recv2,
+    teach_send, teach_recv, logit_send, logit_recv, send1, recv1, send2, recv2, known1, known2,
 ):
     yy, tm, xx = lax.axis_index("inst"), lax.axis_index("tm"), lax.axis_index("filt")
     zz, cc = tm // 2, tm % 2
@@ -58,10 +58,8 @@
     for d in range(1, 4):
         for c in range(2):
             greet((yy, zz * 2 + c, lax.rem(xx + d, nx)))
-    for d in (1, 7, 2, 6, 3, 5, 4):
+    for d in (1, 7, 2, 6):
         greet_y(d)
-    for d in (6, 2, 5, 3, 4):
-        greet_z(d)
 
     start = pl.multiple_of(480 * cc, 16)
     own = pl.ds(pl.multiple_of(PAD + 480 * cc, 16), 480)
@@ -129,7 +127,16 @@
 
     for c in loads:
         c.wait()
-    pl.semaphore_wait(barrier, 35)
+    pl.semaphore_wait(barrier, 19)
+
+    def tell(sem, dev):
+        pl.semaphore_signal(sem, inc=1, device_id=dev, device_id_type=MESH)
+
+    def along_y(d):
+        return (lax.rem(yy + d, ny), tm, xx)
+
+    def along_z(d):
+        return (yy, lax.rem(zz + d, nz) * 2 + cc, xx)
 
     partner = (yy, zz * 2 + oc, xx)
     pair_copies = []
@@ -164,6 +171,8 @@
     for c in teach_copies:
         c.start()
     to_partner(xc, pl.ds(pl.multiple_of(480 + 16 * cc, 16), PAD))
+    for dev in (along_z(7), along_z(1), along_y(2), along_y(6)):
+        tell(known1, dev)
 
     for i in range(4):
         forward(i)
@@ -224,6 +233,10 @@
     to_partner(deriv, pl.ds(start, EPOCH))
     to_partner(deriv, pl.ds(pl.multiple_of(start + 3 * EPOCH, 8), EPOCH))
 
+    pl.semaphore_wait(known1, 4)
+    for dev in (along_z(6), along_z(2)):
+        tell(known2, dev)
+
     pair_copies[1].wait_recv()
     for i in range(4):
         xt[i] = xc[i].T
@@ -316,6 +329,7 @@
         t = jnp.concatenate([grad[pl.ds(288 * y + UNIT * z, UNIT), :] for y, z in units], axis=0)
         tx[slot] = jnp.concatenate([jnp.round(t * factor), power], axis=0).astype(i32).astype(i16)
 
+    pl.semaphore_wait(known2, 2)
     half_y, half_z = yy // 4 == cc, zz // 4
     copies = []
 
@@ -458,6 +472,7 @@
             dma((7,)), dma((2, 4)),
             dma((16,)), dma((16,)),
             dma((8,)), dma((8,)),
+            pltpu.SemaphoreType.REGULAR, pltpu.SemaphoreType.REGULAR,
         ],
         compiler_params=pltpu.CompilerParams(
             collective_id=0, has_side_effects=True, vmem_limit_bytes=63 << 20

time: 38.3 us -> 36.9 us (0.963)
  Pallas kernels: 36.3 us -> 34.9 us
    pallas_call x1, Pallas kernels: 36.3 us -> 34.9 us  [local(): pl.pallas_call(kernel, out_shape=(pltpu.VMEM((4, 4, 5), f32), pltpu.VMEM(...]
where the time goes in v5:
time: 36.9 us; the launch traced here: 36.7 us
  Pallas kernels  34.9 us (95%)
  local copies, waits for them, and re-layouts  1.2 us (3%)
  between operations  0.64 us (2%)
    pallas_call x1, Pallas kernels, local(): pl.pallas_call(kernel, out_shape=(pltpu.VMEM((4, 4, 5), f32), pltpu.VMEM(...  34.9 us
    unnamed x2, local copies, waits for them, and re-layouts  1.2 us

profile of v5, /device:TPU:1, one launch (start us, length us, event | category | flops | bytes accessed | tf_op | source)
XLA Modules:
  0.0 36.7 jit_solution(1557980937914139821)
XLA Ops:
  0.6 34.9 %shard_map.86 = (f32[4,4,5]{2,1,0:T(4,128)S(1)}, f32[18,128]{1,0:T(8,128)S(1)}) custom-call(bf16[4,480,256]{2,1,0:T(8,128)(2,1)} %x.1, bf16[2304,128]{1,0:T(8,128)(2,1)} %w.1, f32[5,128]{1,0:T(8,128)} %bitcast.2, f32[4,4,5]{2,1,0:T(4,128)} %tl_hbm.1, s32[4]{0:T(128)} %night_hbm.1, s32[4,8]{1,0:T(4,128)} %bitcast.3, f32[5]{0:T(128)} %bias_hbm.1), custom_call_target="tpu_custom_call" | custom-call | tf_op jit(solution)/shard_map/pallas_call | solution.py:441
  35.5 0.6 %copy.11 = f32[4,4,5]{2,1,0:T(4,128)} copy(f32[4,4,5]{2,1,0:T(4,128)S(1)} %get-tuple-element.2) | data formatting | bytes 640
  36.1 0.6 %copy.12 = f32[18,128]{1,0:T(8,128)} copy(f32[18,128]{1,0:T(8,128)S(1)} %get-tuple-element.3) | data formatting | bytes 18432

commit v6 on v5

--- a/solution.py
+++ b/solution.py
@@ -114,16 +114,15 @@
             if p < 4:
                 y_taps[i, 2 * p + 1, PAD : PAD + 480, :] = y[:, 128:]
 
-    def finish(i, epochs):
-        for e in epochs:
-            o = PAD - 4 + EPOCH * e
-            pre = y_taps[i, 0, pl.ds(o, EPOCH), :]
-            for k in range(1, 9):
-                pre = pre + y_taps[i, k, pl.ds(o + k, EPOCH), :]
-            ex = jnp.exp(jnp.minimum(pre, 0.0))
-            act = jnp.where(pre > 0, pre, ex - 1.0)
-            deriv[i, pl.ds(pl.multiple_of(start + EPOCH * e, 8), EPOCH), :] = ex
-            pooled[pl.ds(4 * i + e, 1), :] = jnp.sum(act, axis=0, keepdims=True) * (1.0 / EPOCH)
+    def finish(i, at, count):
+        o = PAD - 4 + at
+        pre = y_taps[i, 0, pl.ds(o, count), :]
+        for k in range(1, 9):
+            pre = pre + y_taps[i, k, pl.ds(o + k, count), :]
+        ex = jnp.exp(jnp.minimum(pre, 0.0))
+        act = jnp.where(pre > 0, pre, ex - 1.0)
+        deriv[i, pl.ds(pl.multiple_of(start + at, 8), count), :] = ex
+        return jnp.sum(act, axis=0, keepdims=True) * (1.0 / EPOCH)
 
     for c in loads:
         c.wait()
@@ -176,10 +175,11 @@
 
     for i in range(4):
         forward(i)
-        finish(i, (1, 2))
+        for e, at, count in ((0, 8, EPOCH - 8), (1, EPOCH, EPOCH), (2, 2 * EPOCH, EPOCH), (3, 3 * EPOCH, EPOCH - 8)):
+            pooled[pl.ds(4 * i + e, 1), :] = finish(i, at, count)
 
     to_partner(xc, pl.ds(pl.multiple_of(PAD + 496 * cc, 16), 464))
-    to_partner(deriv, pl.ds(pl.multiple_of(start + EPOCH, 8), 2 * EPOCH))
+    to_partner(deriv, pl.ds(pl.multiple_of(start + 8, 8), 464))
     pair_copies[0].wait_recv()
 
     @pl.when(zz > 0)
@@ -202,7 +202,8 @@
                     y_taps[i, 2 * p + 1, r : r + PAD, :] = y[o : o + PAD, 128:]
 
     for i in range(4):
-        finish(i, (0, 3))
+        for e, at in ((0, 0), (3, 472)):
+            pooled[pl.ds(4 * i + e, 1), :] += finish(i, at, 8)
 
     for c in small[2:]:
         c.wait()
@@ -230,16 +231,16 @@
     for c in logit_copies:
         c.start()
 
-    to_partner(deriv, pl.ds(start, EPOCH))
-    to_partner(deriv, pl.ds(pl.multiple_of(start + 3 * EPOCH, 8), EPOCH))
-
+    to_partner(deriv, pl.ds(start, 8))
+    to_partner(deriv, pl.ds(pl.multiple_of(start + 472, 8), 8))
+
+
+    pair_copies[1].wait_recv()
+    for i in range(4):
+        xt[i] = xc[i].T
     pl.semaphore_wait(known1, 4)
     for dev in (along_z(6), along_z(2)):
         tell(known2, dev)
-
-    pair_copies[1].wait_recv()
-    for i in range(4):
-        xt[i] = xc[i].T
     for d in nearby:
         s = lax.rem(yy + d, ny)
         arrived(teach.at[s], teach_recv.at[s])
@@ -335,7 +336,7 @@
 
     def send(copy, sent):
         copies.append((copy, sent))
-        pl.when(sent)(copy.start)
+        copy.start() if sent is True else pl.when(sent)(copy.start)
 
     far_first = ((2, 0), (3, 1), (1, 3), (0, 2))
     for h in range(2):
@@ -343,10 +344,10 @@
             code(2 * j + h, [(j, j % 2 + 4 * h), (j, j % 2 + 4 * h + 2)])
         for m, (near, far) in enumerate(far_first):
             j = lax.rem(yy + jnp.where(half_y, near, far), 4)
-            dev = (4 * cc + j, zz * 2 + h, xx)
+            dev = (4 * cc + j, zz * 2 + (oc if h else cc), xx)
             send(
                 remote(tx.at[2 * j + h], rx.at[yy], send1.at[4 * h + m], recv1.at[yy], dev),
-                jnp.logical_not((yy == 4 * cc + j) & (cc == h)),
+                True if h else yy != 4 * cc + j,
             )
         for z in range(4 * h, 4 * h + 4):
             code(8 + z, [(1 - z % 2, z), (3 - z % 2, z)])
@@ -360,7 +361,7 @@
 
     @pl.when(half_y)
     def _():
-        rx[yy] = tx[2 * lax.rem(yy, 4) + cc]
+        rx[yy] = tx[2 * lax.rem(yy, 4)]
 
     rx[8 + zz] = tx[8 + zz]
 
@@ -368,7 +369,7 @@
     for k in range(2):
         for m in range(4):
             if k == 0:
-                own, dev = zz, (yy, (yy % 2 + 4 * cc + 2 * (m // 2)) * 2 + m % 2, xx)
+                own, dev = zz, (yy, (yy % 2 + jnp.where(half_y, 0, 4) + 2 * (m // 2)) * 2 + m % 2, xx)
             else:
                 own, dev = yy, (4 * cc + 1 - zz % 2 + 2 * (m // 2), zz * 2 + m % 2, xx)
             slot = 4 * k + m
@@ -400,19 +401,21 @@
             def _():
                 rx2[own] = tx2[slot]
 
-    @pl.when(cc == 0)
+    z_first = jnp.logical_not(half_y) | (zz < 4)
+
+    @pl.when(jnp.logical_not(z_first))
     def _():
         hand_out(0)
         hand_out(1)
 
-    @pl.when(cc == 1)
+    @pl.when(z_first)
     def _():
         hand_out(1)
         hand_out(0)
 
     copies += [(copy, sent) for copy, sent, _ in handed]
     even = (yy + zz) % 2 == 0
-    holder = jnp.where(even, half_z, yy // 4)
+    holder = jnp.where(even & (half_z == 1), 1 - yy // 4, yy // 4)
     place = jnp.where(even, zz, yy)
     for s in range(8):
         @pl.when(jnp.logical_not((place == s) & (holder == cc)))
@@ -431,7 +434,7 @@
     for c in pair_copies + [goal_copy] + teach_copies + logit_copies:
         c.wait_send()
     for c, sent in copies:
-        pl.when(sent)(c.wait_send)
+        c.wait_send() if sent is True else pl.when(sent)(c.wait_send)
 
 
 def local(activations, conv_weight, class_weight, class_bias, teacher_logits, night_of, section_labels):

time: 36.9 us -> 36.7 us (level)
  no operation moved by 1% of the time
where the time goes in v6:
time: 36.7 us; the launch traced here: 36.6 us
  Pallas kernels  34.7 us (95%)
  local copies, waits for them, and re-layouts  1.2 us (3%)
  between operations  0.64 us (2%)
    pallas_call x1, Pallas kernels, local(): pl.pallas_call(kernel, out_shape=(pltpu.VMEM((4, 4, 5), f32), pltpu.VMEM(...  34.7 us
    unnamed x2, local copies, waits for them, and re-layouts  1.2 us

profile of v6, /device:TPU:1, one launch (start us, length us, event | category | flops | bytes accessed | tf_op | source)
XLA Modules:
  0.0 36.6 jit_solution(12577571245690739511)
XLA Ops:
  0.6 34.7 %shard_map.86 = (f32[4,4,5]{2,1,0:T(4,128)S(1)}, f32[18,128]{1,0:T(8,128)S(1)}) custom-call(bf16[4,480,256]{2,1,0:T(8,128)(2,1)} %x.1, bf16[2304,128]{1,0:T(8,128)(2,1)} %w.1, f32[5,128]{1,0:T(8,128)} %bitcast.2, f32[4,4,5]{2,1,0:T(4,128)} %tl_hbm.1, s32[4]{0:T(128)} %night_hbm.1, s32[4,8]{1,0:T(4,128)} %bitcast.3, f32[5]{0:T(128)} %bias_hbm.1), custom_call_target="tpu_custom_call" | custom-call | tf_op jit(solution)/shard_map/pallas_call | solution.py:444
  35.4 0.6 %copy.11 = f32[4,4,5]{2,1,0:T(4,128)} copy(f32[4,4,5]{2,1,0:T(4,128)S(1)} %get-tuple-element.2) | data formatting | bytes 640
  36.0 0.6 %copy.12 = f32[18,128]{1,0:T(8,128)} copy(f32[18,128]{1,0:T(8,128)S(1)} %get-tuple-element.3) | data formatting | bytes 18432

commit v7 on v6

--- a/solution.py
+++ b/solution.py
@@ -124,8 +124,6 @@
         deriv[i, pl.ds(pl.multiple_of(start + at, 8), count), :] = ex
         return jnp.sum(act, axis=0, keepdims=True) * (1.0 / EPOCH)
 
-    for c in loads:
-        c.wait()
     pl.semaphore_wait(barrier, 19)
 
     def tell(sem, dev):
@@ -140,18 +138,18 @@
     partner = (yy, zz * 2 + oc, xx)
     pair_copies = []
 
-    def to_partner(ref, rows):
+    def to_partner(ref, rows, src=None):
         k = len(pair_copies)
-        c = remote(ref.at[:, rows], ref.at[:, rows], pair_send.at[k], pair_recv.at[k], partner)
+        c = remote(ref.at[:, rows] if src is None else src, ref.at[:, rows], pair_send.at[k], pair_recv.at[k], partner)
         c.start()
         pair_copies.append(c)
 
-    halo_src = pl.ds(pl.multiple_of(PAD + 944 * cc, 16), PAD)
+    halo_src = pl.ds(pl.multiple_of(464 * cc, 16), PAD)
     halo_dst = pl.ds(pl.multiple_of((PAD + 960) * oc, 16), PAD)
     has_next = jnp.where(cc == 0, zz > 0, zz < nz - 1)
     halo_copies = [
         remote(
-            xc.at[:, halo_src], xc.at[:, halo_dst], halo_send.at[c], halo_recv.at[oc],
+            x.at[:, halo_src], xc.at[:, halo_dst], halo_send.at[c], halo_recv.at[oc],
             (yy, (zz - 1 + 2 * cc) * 2 + c, xx),
         )
         for c in range(2)
@@ -169,10 +167,12 @@
     ]
     for c in teach_copies:
         c.start()
-    to_partner(xc, pl.ds(pl.multiple_of(480 + 16 * cc, 16), PAD))
+    to_partner(xc, pl.ds(pl.multiple_of(480 + 16 * cc, 16), PAD), x.at[:, pl.ds(pl.multiple_of(464 * oc, 16), PAD)])
     for dev in (along_z(7), along_z(1), along_y(2), along_y(6)):
         tell(known1, dev)
 
+    for c in loads:
+        c.wait()
     for i in range(4):
         forward(i)
         for e, at, count in ((0, 8, EPOCH - 8), (1, EPOCH, EPOCH), (2, 2 * EPOCH, EPOCH), (3, 3 * EPOCH, EPOCH - 8)):

time: 36.7 us -> 36.9 us (level)
  no operation moved by 1% of the time
where the time goes in v7:
time: 36.9 us; the launch traced here: 36.8 us
  Pallas kernels  34.9 us (95%)
  local copies, waits for them, and re-layouts  1.2 us (3%)
  between operations  0.64 us (2%)
    pallas_call x1, Pallas kernels, local(): pl.pallas_call(kernel, out_shape=(pltpu.VMEM((4, 4, 5), f32), pltpu.VMEM(...  34.9 us
    unnamed x2, local copies, waits for them, and re-layouts  1.2 us

profile of v7, /device:TPU:1, one launch (start us, length us, event | category | flops | bytes accessed | tf_op | source)
XLA Modules:
  0.0 36.8 jit_solution(15041379712561277006)
XLA Ops:
  0.6 34.9 %shard_map.86 = (f32[4,4,5]{2,1,0:T(4,128)S(1)}, f32[18,128]{1,0:T(8,128)S(1)}) custom-call(bf16[4,480,256]{2,1,0:T(8,128)(2,1)} %x.1, bf16[2304,128]{1,0:T(8,128)(2,1)} %w.1, f32[5,128]{1,0:T(8,128)} %bitcast.2, f32[4,4,5]{2,1,0:T(4,128)} %tl_hbm.1, s32[4]{0:T(128)} %night_hbm.1, s32[4,8]{1,0:T(4,128)} %bitcast.3, f32[5]{0:T(128)} %bias_hbm.1), custom_call_target="tpu_custom_call" | custom-call | tf_op jit(solution)/shard_map/pallas_call | solution.py:444
  35.6 0.6 %copy.11 = f32[4,4,5]{2,1,0:T(4,128)} copy(f32[4,4,5]{2,1,0:T(4,128)S(1)} %get-tuple-element.2) | data formatting | bytes 640
  36.2 0.6 %copy.12 = f32[18,128]{1,0:T(8,128)} copy(f32[18,128]{1,0:T(8,128)S(1)} %get-tuple-element.3) | data formatting | bytes 18432
